TPU v7x, 256 devices: a whole 4x4x8 slice. The times are simulated.
256 devices in a mesh: vox: 32 (over z, y), col: 8 (over x, core).
Axes of the slice: x: 4, y: 4, z: 8, core: 2. Of those that a mesh axis runs over, the one named last changes fastest.
Arguments:
- start_modes: float32 [128, 131072], P('col', 'vox'), may hold values from -48 to 48
- start_dirs: float32 [128, 131072], P('col', 'vox'), may hold values from -6 to 6
- coupling: float32 [13, 131072], P(None, ('vox', 'col')), may hold values from 0.05 to 1
- relax_class: int32 [131072], P(('vox', 'col')), may hold values from 0 to 3
- relaxivity: float32 [4], replicated, may hold values from 0.5 to 4
Outputs:
- modes: float32 [128, 131072], P('col', 'vox')
- ritz: float32 [128, 128], replicated
All inputs are finite; a program needn't handle non-finite values.
Results may differ from a plain program's by a relative error of at most 0.0003.
Values sent between devices are 32-bit elements; how exact they have to be, the bound alone decides.
A program may use at most 64 MiB of HBM per device.

v0:
```python
import math

import jax
import jax.numpy as jnp
from jax import lax
from jax.sharding import PartitionSpec as P

NX = 256
NZ = 2
HALF = 13
ITERS = 2
QSTEPS = 3


offsets = [
    (a, b, c) for a in (-1, 0, 1) for b in (-1, 0, 1) for c in (-1, 0, 1) if (a, b, c) > (0, 0, 0)
]


def from_behind(block, axis, distance):
    devices = range(lax.axis_size(axis))
    route = [(i - distance, i) for i in devices if i - distance in devices]
    return lax.ppermute(block, axis, route)


def extended_2(block, sides, width):
    for axis, dim in sides:
        count = lax.axis_size(axis)
        forward = [(i, i + 1) for i in range(count - 1)]
        backward = [(target, source) for source, target in forward]
        low = lax.ppermute(
            lax.slice_in_dim(block, block.shape[dim] - width, None, axis=dim), axis, forward
        )
        high = lax.ppermute(lax.slice_in_dim(block, 0, width, axis=dim), axis, backward)
        block = jnp.concatenate([low, block, high], axis=dim)
    return block


def matmul(left, right):
    return jnp.dot(left, right, precision=lax.Precision.HIGHEST, preferred_element_type=jnp.float32)


def lower_solve(lower, rhs):
    return lax.linalg.triangular_solve(lower, rhs, left_side=True, lower=True)


def upper_solve(lower, rhs):
    return lax.linalg.triangular_solve(lower, rhs, left_side=True, lower=True, transpose_a=True)


def symmetric(matrix):
    return 0.5 * (matrix + matrix.T)


def project_pencil(gram_a, gram_b, count):
    sym_a = symmetric(gram_a)
    scales = lax.rsqrt(jnp.diagonal(gram_b) + 1e-06)
    normed_b = scales[:, None] * gram_b * scales[None, :]
    normed_a = scales[:, None] * sym_a * scales[None, :]
    lower = jnp.linalg.cholesky(normed_b)
    half_way = lower_solve(lower, normed_a)
    reduced = lower_solve(lower, half_way.T)
    shift = 2.0 * jnp.max(jnp.sum(jnp.abs(reduced), axis=1))
    iterate = jnp.eye(gram_a.shape[0], count, dtype=jnp.float32)
    for sweep_index in range(QSTEPS):
        iterate = shift * iterate - matmul(reduced, iterate)
        factor = jnp.linalg.cholesky(matmul(iterate.T, iterate))
        iterate = lower_solve(factor, iterate.T).T
    return scales[:, None] * upper_solve(lower, iterate)


def neighbour_sum(padded, coupled):
    rows_y = padded.shape[1] - 2
    rows_z = padded.shape[2] - 2
    rows_x = padded.shape[3] - 2
    total = jnp.zeros((padded.shape[0], rows_y, rows_z, rows_x), jnp.float32)
    for which, (step_y, step_z, step_x) in enumerate(offsets):
        ahead = padded[
            :,
            1 + step_y : 1 + step_y + rows_y,
            1 + step_z : 1 + step_z + rows_z,
            1 + step_x : 1 + step_x + rows_x,
        ]
        behind = padded[
            :,
            1 - step_y : 1 - step_y + rows_y,
            1 - step_z : 1 - step_z + rows_z,
            1 - step_x : 1 - step_x + rows_x,
        ]
        here = coupled[which, 1 : 1 + rows_y, 1 : 1 + rows_z, 1 : 1 + rows_x]
        back = coupled[
            which,
            1 - step_y : 1 - step_y + rows_y,
            1 - step_z : 1 - step_z + rows_z,
            1 - step_x : 1 - step_x + rows_x,
        ]
        total = total + here[None] * ahead
        total = total + back[None] * behind
    return total


def pad_plane(array):
    return jnp.pad(array, ((0, 0), (0, 0), (1, 1), (1, 1)))


def quotient(modes, images):
    total = lax.psum(matmul(modes, images.T), ("vox", "col"))
    return symmetric(total)


def on_device(start_modes, start_dirs, coupling, relax_class, relaxivity):
    local_voxels = coupling.shape[1]
    match = relax_class[:, None] == jnp.arange(relaxivity.shape[0], dtype=jnp.int32)[None, :]
    voxel_rate = jnp.sum(jnp.where(match, relaxivity[None, :], jnp.float32(0.0)), axis=1)
    damping = 1.0 / (1.0 + voxel_rate)
    own_coupling = coupling.reshape(HALF, 1, NZ, NX)
    before = from_behind(own_coupling, ("vox", "col"), 1)
    coupled = pad_plane(
        jnp.concatenate([before, own_coupling, jnp.zeros_like(own_coupling)], axis=1)
    )
    position = lax.axis_index(("vox", "col"))
    device_count = lax.axis_size(("vox", "col"))
    plane = jnp.ones((1, 1, NZ, NX), jnp.float32)
    upper_flag = (position > 0).astype(jnp.float32)
    lower_flag = (position < device_count - 1).astype(jnp.float32)
    unity = pad_plane(jnp.concatenate([upper_flag * plane, plane, lower_flag * plane], axis=1))
    degree = neighbour_sum(unity, coupled).reshape(local_voxels)
    diagonal = degree + voxel_rate

    def operate(field):
        count = field.shape[0]
        shaped = field.reshape(count, 1, NZ, NX)
        extended = extended_2(shaped, ((("vox", "col"), 1),), 1)
        padded = pad_plane(extended)
        return diagonal[None, :] * field - neighbour_sum(padded, coupled).reshape(
            count, local_voxels
        )

    modes, dirs = (
        lax.all_to_all(start_modes, "col", split_axis=1, concat_axis=0, tiled=True),
        lax.all_to_all(start_dirs, "col", split_axis=1, concat_axis=0, tiled=True),
    )
    count = modes.shape[0]
    images = operate(modes)
    dir_images = operate(dirs)
    ritz = quotient(modes, images)
    for iteration in range(ITERS):
        resid = images - matmul(ritz, modes)
        search = resid * damping[None, :]
        search_images = operate(search)
        basis = jnp.concatenate([modes, search, dirs], axis=0)
        basis_images = jnp.concatenate([images, search_images, dir_images], axis=0)
        local_a = matmul(basis, basis_images.T)
        local_b = matmul(basis, basis.T)
        gram_a, gram_b = lax.psum((local_a, local_b), ("vox", "col"))
        coeffs = project_pencil(gram_a, gram_b, count)
        modes = matmul(coeffs.T, basis)
        images = matmul(coeffs.T, basis_images)
        dirs = matmul(coeffs[count:].T, basis[count:])
        dir_images = matmul(coeffs[count:].T, basis_images[count:])
        ritz = quotient(modes, images)
    total_voxels = device_count * local_voxels
    scaled = modes * math.sqrt(total_voxels)
    modes_out = lax.all_to_all(scaled, "col", split_axis=0, concat_axis=1, tiled=True)
    return (modes_out, ritz)


def solution(mesh):
    in_specs = (P("col", "vox"), P("col", "vox"), P(None, ("vox", "col")), P(("vox", "col")), P())
    out_specs = (P("col", "vox"), P())
    return jax.shard_map(
        on_device, mesh=mesh, in_specs=in_specs, out_specs=out_specs, check_vma=False
    )
```

profile of v0, /device:TPU:1, one launch (start us, length us, event | category | flops | bytes accessed | tf_op | source)
XLA Modules:
  0.0 1733.3 jit_solution(11976527018198322847)
XLA Ops:
  8.8 6.6 all-to-all-start
  16.2 3.5 collective-permute-start
  25.2 4.1 all-to-all-start.1
  31.4 3.6 collective-permute-start.1
  36.0 2.9 collective-permute-start.6
  38.9 2.6 collective-permute-start.5
  41.6 2.3 select_maximum_fusion.6
  43.9 4.5 multiply_subtract_fusion.3
  49.6 3.4 select_maximum_fusion.2
  53.1 245.1 %all-reduce.15.cloned.1.call-done = f32[128,128]{0,1:T(8,128)} async-done(((f32[128,128]{0,1:T(8,128)}), f32[128,128]{0,1:T(8,128)}) %all-reduce.15.cloned.1.call-update) | async-done | bytes 65552 | tf_op jit(solution)/shard_map/psum | solution.py:107
  303.3 3.9 collective-permute-start.3
  307.2 5.4 fusion.64
  317.3 4.4 fusion.89
  325.0 256.1 %all-reduce.23.cloned.1.call-done = (f32[384,384]{1,0:T(8,128)}, f32[384,384]{0,1:T(8,128)}) async-done(((f32[384,384]{1,0:T(8,128)}, f32[384,384]{0,1:T(8,128)}), (f32[384,384]{1,0:T(8,128)}, f32[384,384]{0,1:T(8,128)})) %all-reduce.23.cloned.1.call-update) | async-done | bytes 1179664 | tf_op jit(solution)/shard_map/psum | solution.py:155
  581.2 6.6 gather_fusion
  590.4 11.7 cholesky.310
  602.2 9.8 custom-call.40
  614.4 11.7 cholesky.329
  626.2 9.9 custom-call.41
  637.5 11.7 cholesky.348
  652.6 5.9 while.12
  658.5 29.7 %custom-call.47 = f32[3,128,128]{1,2,0:T(8,128)S(1)} custom-call(f32[3,128,128]{2,1,0:T(8,128)S(1)} %get-tuple-element.49), custom_call_target="InvertDiagBlocksLowerTriangular" | custom-call | tf_op jit(solution)/shard_map/triangular_solve/custom-call.8 | solution.py:48
  695.7 11.7 cholesky.361
  708.7 9.8 custom-call.44
  720.8 11.7 cholesky.372
  733.9 9.8 custom-call.45
  745.5 11.9 cholesky.383
  758.7 9.8 custom-call.46
  773.6 237.5 %all-reduce.17.cloned.1.call-done = f32[128,128]{1,0:T(8,128)} async-done(((f32[128,128]{1,0:T(8,128)}), f32[128,128]{1,0:T(8,128)}) %all-reduce.17.cloned.1.call-update) | async-done | bytes 65552 | tf_op jit(solution)/shard_map/psum | solution.py:107
  1015.4 3.6 collective-permute-start.7
  1024.6 4.4 fusion.39
  1031.5 259.7 %all-reduce.21.cloned.1.call-done = (f32[384,384]{1,0:T(8,128)}, f32[384,384]{0,1:T(8,128)}) async-done(((f32[384,384]{1,0:T(8,128)}, f32[384,384]{0,1:T(8,128)}), (f32[384,384]{1,0:T(8,128)}, f32[384,384]{0,1:T(8,128)})) %all-reduce.21.cloned.1.call-update) | async-done | bytes 1179664 | tf_op jit(solution)/shard_map/psum | solution.py:155
  1291.2 6.6 gather_fusion.1
  1300.6 11.7 cholesky.396
  1312.4 9.8 custom-call.48
  1324.5 11.7 cholesky.415
  1336.3 10.2 custom-call.49
  1347.8 11.7 cholesky.434
  1363.5 6.4 while.13
  1369.9 29.7 %custom-call.55 = f32[3,128,128]{1,2,0:T(8,128)S(1)} custom-call(f32[3,128,128]{2,1,0:T(8,128)S(1)} %get-tuple-element.52), custom_call_target="InvertDiagBlocksLowerTriangular" | custom-call | tf_op jit(solution)/shard_map/triangular_solve/custom-call.8 | solution.py:48
  1407.1 11.7 cholesky.447
  1420.1 9.8 custom-call.52
  1432.0 11.7 cholesky.458
  1445.0 9.8 custom-call.53
  1456.7 11.9 cholesky.469
  1470.0 9.8 custom-call.54
  1485.0 7.1 all-to-all-start.2
  1492.1 231.0 %all-reduce.19.cloned.1.call-done = f32[128,128]{1,0:T(8,128)} async-done(((f32[128,128]{1,0:T(8,128)}), f32[128,128]{1,0:T(8,128)}) %all-reduce.19.cloned.1.call-update) | async-done | bytes 65552 | tf_op jit(solution)/shard_map/psum | solution.py:107
  (329 shorter events, 108.3 us)
Async XLA Ops:
  8.8 16.4 all-to-all-start
  16.2 8.8 collective-permute-start
  25.2 10.6 all-to-all-start.1
  29.3 268.9 %all-reduce.15.cloned.1.call-start = ((), (), s32[]{:S(2)}) async-start(), calls=%async_computation.3 | async-start | bytes 131072 | tf_op jit(solution)/shard_map/psum | solution.py:107
  29.5 12.1 collective-permute-start.2
  31.4 10.1 collective-permute-start.1
  35.1 13.3 copy-start.21
  35.1 13.3 copy-start.23
  35.1 13.3 copy-start.25
  35.1 13.3 copy-start.27
  35.2 13.3 copy-start.29
  35.2 13.3 copy-start.31
  35.2 13.3 copy-start.33
  35.8 17.2 copy-start.35
  36.0 12.5 copy-start.15
  36.0 13.6 collective-permute-start.6
  38.9 10.7 collective-permute-start.5
  49.6 531.6 %all-reduce.23.cloned.1.call-start = ((), (), s32[]{:S(2)}) async-start(), calls=%async_computation.7 | async-start | bytes 2359296 | tf_op jit(solution)/shard_map/psum | solution.py:155
  301.3 13.6 copy-start.16
  301.3 13.6 collective-permute-start.4
  303.3 11.6 collective-permute-start.3
  312.6 4.6 copy-start.22
  312.6 4.6 copy-start.24
  312.6 4.6 copy-start.26
  312.6 4.6 copy-start.28
  325.0 686.1 %all-reduce.17.cloned.1.call-start = ((), (), s32[]{:S(2)}) async-start(), calls=%async_computation.4 | async-start | bytes 131072 | tf_op jit(solution)/shard_map/psum | solution.py:107
  581.2 6.6 copy-start.2
  581.2 7.7 copy-start
  590.4 11.7 copy-start.12
  744.1 26.5 %copy-start.7 = (f32[128,512]{1,0:T(8,128)S(1)}, f32[128,512]{1,0:T(8,128)}, u32[]{:S(2)}) copy-start(f32[128,512]{1,0:T(8,128)} %copy-done.6) | copy-start | bytes 786436
  744.1 26.5 %copy-start.9 = (f32[128,512]{1,0:T(8,128)S(1)}, f32[128,512]{1,0:T(8,128)}, u32[]{:S(2)}) copy-start(f32[128,512]{1,0:T(8,128)} %copy-done.8) | copy-start | bytes 786436
  770.2 241.8 %copy-start.37 = (f32[512]{0:T(512)S(1)}, f32[512]{0:T(512)}, u32[]{:S(2)}) copy-start(f32[512]{0:T(512)} %get-tuple-element.163) | copy-start | bytes 6148
  771.3 257.8 %copy-start.4 = (f32[128,512]{1,0:T(8,128)}, f32[128,512]{1,0:T(8,128)S(1)}, u32[]{:S(2)}) copy-start(f32[128,512]{1,0:T(8,128)S(1)} %fusion.13) | copy-start | bytes 786436
  773.1 518.2 %all-reduce.21.cloned.1.call-start = ((), (), s32[]{:S(2)}) async-start(), calls=%async_computation.6 | async-start | bytes 2359296 | tf_op jit(solution)/shard_map/psum | solution.py:155
  773.6 255.6 %copy-start.10 = (f32[128,512]{1,0:T(8,128)}, f32[128,512]{1,0:T(8,128)S(1)}, u32[]{:S(2)}) copy-start(f32[128,512]{1,0:T(8,128)S(1)} %fusion.15) | copy-start | bytes 786436
  1013.5 8.3 collective-permute-start.8
  1015.4 6.9 collective-permute-start.7
  1019.5 9.7 copy-start.17
  1029.2 268.7 %copy-start.19 = (f32[128,512]{1,0:T(8,128)}, f32[128,512]{1,0:T(8,128)S(1)}, u32[]{:S(2)}) copy-start(f32[128,512]{1,0:T(8,128)S(1)} %multiply_subtract_fusion) | copy-start | bytes 786436
  1031.5 691.6 %all-reduce.19.cloned.1.call-start = ((), (), s32[]{:S(2)}) async-start(), calls=%async_computation.5 | async-start | bytes 131072 | tf_op jit(solution)/shard_map/psum | solution.py:107
  1291.2 6.7 copy-start.3
  1291.2 7.7 copy-start.1
  1300.5 11.7 copy-start.13
  1454.8 26.9 %copy-start.11 = (f32[128,512]{1,0:T(8,128)S(1)}, f32[128,512]{1,0:T(8,128)}, u32[]{:S(2)}) copy-start(f32[128,512]{1,0:T(8,128)} %copy-done.10) | copy-start | bytes 786436
  1455.9 27.2 %copy-start.5 = (f32[128,512]{1,0:T(8,128)S(1)}, f32[128,512]{1,0:T(8,128)}, u32[]{:S(2)}) copy-start(f32[128,512]{1,0:T(8,128)} %copy-done.4) | copy-start | bytes 786436
  1455.9 27.2 %copy-start.18 = (f32[128,512]{1,0:T(8,128)S(1)}, f32[128,512]{1,0:T(8,128)}, u32[]{:S(2)}) copy-start(f32[128,512]{1,0:T(8,128)} %copy-done.17) | copy-start | bytes 786436
  1455.9 27.2 %copy-start.20 = (f32[128,512]{1,0:T(8,128)S(1)}, f32[128,512]{1,0:T(8,128)}, u32[]{:S(2)}) copy-start(f32[128,512]{1,0:T(8,128)} %copy-done.19) | copy-start | bytes 786436
  1485.0 240.7 %all-to-all-start.2 = ((f32[8,16,512]{2,1,0:T(8,128)}), f32[8,16,512]{2,1,0:T(8,128)S(1)}, u32[]{:S(2)}, u32[]{:S(2)}) async-start(f32[8,16,512]{2,1,0:T(8,128)} %bitcast.87), calls=%async_computation.2 | async-start | bytes 524288 | tf_op jit(solution)/shard_map/all_to_all | solution.py:164
  (7 other events, 23.2 us)
Sparse Core Ops, SparseCore 0:
  49.7 248.4 all-reduce.14
  325.1 256.0 all-reduce.22
  773.2 237.8 all-reduce.16
  1031.6 259.5 all-reduce.20
  1485.1 237.9 all-reduce.18
where the time goes:
time: 1740 us; the launch traced here: 1730 us
  waiting for transfers between devices  1230 us (71%)
  other arithmetic  348 us (20%)
  matrix products  48.7 us (3%)
  starting transfers between devices  44.1 us (3%)
  local copies, waits for them, and re-layouts  41.4 us (2%)
  between operations  21 us (1%)
    psum x3, waiting for transfers between devices, quotient(): total = lax.psum(matmul(modes, images.T), ('vox', 'col'))  714 us
    psum x2, waiting for transfers between devices, on_device(): gram_a, gram_b = lax.psum((local_a, local_b), ('vox', 'col'))  516 us
    another operation x21, other arithmetic, project_pencil(): lower = jnp.linalg.cholesky(normed_b)  114 us
    another operation x18, other arithmetic, project_pencil(): factor = jnp.linalg.cholesky(matmul(iterate.T, iterate))  74.7 us
    another operation x12, other arithmetic, lower_solve(): return lax.linalg.triangular_solve(lower, rhs, left_side=True, lower=True)  62.8 us
    another operation x5, other arithmetic, upper_solve(): lax.linalg.triangular_solve(lower, rhs, left_side=True, lower=True, trans...  59.5 us
  transfers between devices with their start and end apart: 17, of which 6 were waited for; matrix products, arithmetic and copies ran while one was open for 2% of the time, Pallas kernels for 0%

commit v1 on v0

--- a/solution.py
+++ b/solution.py
@@ -1,8 +1,11 @@
+import functools
 import math
 
 import jax
 import jax.numpy as jnp
 from jax import lax
+from jax.experimental import pallas as pl
+from jax.experimental.pallas import tpu as pltpu
 from jax.sharding import PartitionSpec as P
 
 NX = 256
@@ -10,6 +13,169 @@
 HALF = 13
 ITERS = 2
 QSTEPS = 3
+
+
+SIZES = {"core": 2, "x": 4, "y": 4, "z": 8}
+
+
+def digit(axis):
+    if axis in ("core", "x"):
+        c = lax.axis_index("col")
+        return lax.rem(c, 2) if axis == "core" else lax.div(c, 2)
+    v = lax.axis_index("vox")
+    return lax.rem(v, 4) if axis == "y" else lax.div(v, 4)
+
+
+def peer(axis, step):
+    size = SIZES[axis]
+    other = lax.rem(digit(axis) + step, size)
+    if axis == "core":
+        return {"col": digit("x") * 2 + other}
+    if axis == "x":
+        return {"col": other * 2 + digit("core")}
+    if axis == "y":
+        return {"vox": digit("z") * 4 + other}
+    return {"vox": other * 4 + digit("y")}
+
+
+def greet(axes):
+    barrier = pltpu.get_barrier_semaphore()
+    count = 0
+    for axis in axes:
+        for step in range(1, SIZES[axis]):
+            pl.semaphore_signal(barrier, inc=1, device_id=peer(axis, step), device_id_type=pl.DeviceIdType.MESH)
+            count += 1
+    pl.semaphore_wait(barrier, count)
+
+
+class Part:
+    def __init__(self, start, rows, stages):
+        self.start, self.rows, self.stages = start, rows, stages
+
+    def plan(self, scratch):
+        self.steps = []
+        rows = self.rows
+        for axis, kind in self.stages:
+            size = SIZES[axis]
+            if kind == "scatter":
+                rows = rows // size
+            land = len(scratch)
+            scratch.append(pltpu.VMEM((size, rows, 128), jnp.float32))
+            held = len(scratch)
+            scratch.append(pltpu.VMEM((rows, 128), jnp.float32))
+            self.steps.append((axis, kind, rows, land, held))
+        self.gathers = [s for s in self.steps if s[1] == "scatter"][::-1]
+
+
+def sum_kernel(parts, axes, ncopies, in_ref, out_ref, *scratch):
+    send, recv = scratch[-2], scratch[-1]
+    greet(axes)
+    copies = []
+
+    def launch(src, dst, axis, step):
+        k = len(copies)
+        copy = pltpu.make_async_remote_copy(src_ref=src, dst_ref=dst, send_sem=send.at[k], recv_sem=recv.at[k],
+                                            device_id=peer(axis, step), device_id_type=pl.DeviceIdType.MESH)
+        copy.start()
+        copies.append(copy)
+        return copy
+
+    state = []
+    for part in parts:
+        state.append({"ref": in_ref, "at": part.start, "start": part.start, "rows": part.rows, "waiting": None})
+
+    def begin(part, st, s):
+        if s < len(part.steps):
+            axis, kind, rows, land, held = part.steps[s]
+            size = SIZES[axis]
+            me = digit(axis)
+            waiting = []
+            for step in range(1, size):
+                if kind == "scatter":
+                    other = lax.rem(me + step, size)
+                    src = st["ref"].at[pl.ds(pl.multiple_of(st["at"] + other * rows, 8), rows)]
+                else:
+                    src = st["ref"].at[pl.ds(pl.multiple_of(st["at"], 8), rows)]
+                waiting.append(launch(src, scratch[land].at[step], axis, step))
+            st["waiting"] = waiting
+        else:
+            g = s - len(part.steps)
+            axis, kind, rows, land, held = part.gathers[g]
+            mine = out_ref.at[pl.ds(pl.multiple_of(st["start"], 8), rows)]
+            st["waiting"] = [launch(mine, mine, axis, step) for step in range(1, SIZES[axis])]
+
+    def finish(part, st, s):
+        if s < len(part.steps):
+            axis, kind, rows, land, held = part.steps[s]
+            size = SIZES[axis]
+            me = digit(axis)
+            landing = scratch[land]
+            for copy in st["waiting"]:
+                copy.wait_recv()
+            if kind == "scatter":
+                at = pl.multiple_of(st["at"] + me * rows, 8)
+                total = st["ref"][pl.ds(at, rows)]
+                for step in range(1, size):
+                    total = total + landing[step]
+                st["start"] = st["start"] + me * rows
+            else:
+                landing[0] = st["ref"][pl.ds(pl.multiple_of(st["at"], 8), rows)]
+                total = landing[me]
+                for k in range(1, size):
+                    total = total + landing[lax.rem(me - k + size, size)]
+            if s == len(part.steps) - 1:
+                out_ref[pl.ds(pl.multiple_of(st["start"], 8), rows)] = total
+            else:
+                scratch[held][...] = total
+                st["ref"], st["at"] = scratch[held], 0
+        else:
+            axis, kind, rows, land, held = part.gathers[s - len(part.steps)]
+            for copy in st["waiting"]:
+                copy.wait_recv()
+            st["start"] = st["start"] - digit(axis) * rows
+
+    lengths = [len(p.steps) + len(p.gathers) for p in parts]
+    for part, st in zip(parts, state):
+        begin(part, st, 0)
+    for s in range(max(lengths)):
+        for part, st, n in zip(parts, state, lengths):
+            if s < n:
+                finish(part, st, s)
+                if s + 1 < n:
+                    begin(part, st, s + 1)
+    for copy in copies:
+        copy.wait_send()
+
+
+def all_sum(array, layout, collective_id, name):
+    parts = [Part(*p) for p in layout]
+    scratch = []
+    for p in parts:
+        p.plan(scratch)
+    axes = []
+    ncopies = 0
+    for p in parts:
+        for axis, kind, *_ in p.steps:
+            if axis not in axes:
+                axes.append(axis)
+            ncopies += (SIZES[axis] - 1) * (2 if kind == "scatter" else 1)
+    scratch += [pltpu.SemaphoreType.DMA((ncopies,)), pltpu.SemaphoreType.DMA((ncopies,))]
+    return pl.pallas_call(
+        functools.partial(sum_kernel, parts, axes, ncopies),
+        out_shape=jax.ShapeDtypeStruct(array.shape, jnp.float32),
+        in_specs=[pl.BlockSpec(memory_space=pltpu.VMEM)],
+        out_specs=pl.BlockSpec(memory_space=pltpu.VMEM),
+        scratch_shapes=scratch,
+        compiler_params=pltpu.CompilerParams(collective_id=collective_id, has_side_effects=True,
+                                             vmem_limit_bytes=32 << 20),
+        name=name,
+    )(array)
+
+RITZ_LAYOUT = [(0, 128, [("z", "scatter"), ("core", "exchange"), ("x", "exchange"), ("y", "exchange")])]
+GRAM_LAYOUT = [
+    (0, 768, [("core", "scatter"), ("x", "scatter"), ("y", "scatter"), ("z", "exchange")]),
+    (768, 768, [("core", "scatter"), ("y", "scatter"), ("x", "scatter"), ("z", "exchange")]),
+]
 
 
 offsets = [
@@ -63,10 +229,11 @@
     shift = 2.0 * jnp.max(jnp.sum(jnp.abs(reduced), axis=1))
     iterate = jnp.eye(gram_a.shape[0], count, dtype=jnp.float32)
     for sweep_index in range(QSTEPS):
-        iterate = shift * iterate - matmul(reduced, iterate)
-        factor = jnp.linalg.cholesky(matmul(iterate.T, iterate))
-        iterate = lower_solve(factor, iterate.T).T
-    return scales[:, None] * upper_solve(lower, iterate)
+        iterate = iterate - matmul(reduced, iterate) / shift
+    factor = jnp.linalg.cholesky(matmul(iterate.T, iterate))
+    iterate = lower_solve(factor, iterate.T).T
+    coeffs = scales[:, None] * upper_solve(lower, iterate)
+    return coeffs, symmetric(matmul(coeffs.T, matmul(sym_a, coeffs)))
 
 
 def neighbour_sum(padded, coupled):
@@ -104,8 +271,21 @@
 
 
 def quotient(modes, images):
-    total = lax.psum(matmul(modes, images.T), ("vox", "col"))
-    return symmetric(total)
+    return symmetric(all_sum(matmul(modes, images.T), RITZ_LAYOUT, 1, "ritz_sum"))
+
+
+def gram_blocks(left, right):
+    return [matmul(left[0], jnp.concatenate(right[:1]).T), matmul(left[1], jnp.concatenate(right[:2]).T),
+            matmul(left[2], jnp.concatenate(right).T)]
+
+
+def stacked(rows):
+    return jnp.concatenate([row[:, 128 * k:128 * (k + 1)] for row in rows for k in range(row.shape[1] // 128)])
+
+
+def unstacked(array):
+    b = [array[128 * k:128 * (k + 1)] for k in range(6)]
+    return jnp.block([[b[0], b[1].T, b[3].T], [b[1], b[2], b[4].T], [b[3], b[4], b[5]]])
 
 
 def on_device(start_modes, start_dirs, coupling, relax_class, relaxivity):
@@ -150,15 +330,15 @@
         search_images = operate(search)
         basis = jnp.concatenate([modes, search, dirs], axis=0)
         basis_images = jnp.concatenate([images, search_images, dir_images], axis=0)
-        local_a = matmul(basis, basis_images.T)
-        local_b = matmul(basis, basis.T)
-        gram_a, gram_b = lax.psum((local_a, local_b), ("vox", "col"))
-        coeffs = project_pencil(gram_a, gram_b, count)
+        fields = [modes, search, dirs]
+        local_a = stacked(gram_blocks(fields, [images, search_images, dir_images]))
+        local_b = stacked(gram_blocks(fields, fields))
+        summed = all_sum(jnp.concatenate([local_a, local_b]), GRAM_LAYOUT, 2, "gram_sum")
+        coeffs, ritz = project_pencil(unstacked(summed[:768]), unstacked(summed[768:]), count)
         modes = matmul(coeffs.T, basis)
         images = matmul(coeffs.T, basis_images)
         dirs = matmul(coeffs[count:].T, basis[count:])
         dir_images = matmul(coeffs[count:].T, basis_images[count:])
-        ritz = quotient(modes, images)
     total_voxels = device_count * local_voxels
     scaled = modes * math.sqrt(total_voxels)
     modes_out = lax.all_to_all(scaled, "col", split_axis=0, concat_axis=1, tiled=True)

time: 1740 us -> 513 us (0.29)
  waiting for transfers between devices: 1230 us -> 9.57 us
  Pallas kernels: 0 us -> 98.8 us
  other arithmetic: 348 us -> 262 us
    psum x5 -> x0, waiting for transfers between devices: 1230 us -> none  [the longest x3 714 us: quotient(): total = lax.psum(matmul(modes, images.T), ('vox', 'col'))]
    pallas_call x0 -> x3, Pallas kernels: none -> 98.8 us  [all_sum(): pl.pallas_call(functools.partial(sum_kernel, parts, axes, ncopies), out_s...]
    another operation x18 -> x6, other arithmetic: 74.7 us -> 25.7 us  [project_pencil(): factor = jnp.linalg.cholesky(matmul(iterate.T, iterate))]
    another operation x12 -> x4, other arithmetic: 62.8 us -> 23.4 us  [lower_solve(): return lax.linalg.triangular_solve(lower, rhs, left_side=True, lower=True)]
  transfers between devices with their start and end apart: 17 -> 12, of which waited for: 6 -> 4; matrix products, arithmetic and copies ran while one was open for 2% -> 5% of each run, Pallas kernels for 0% -> 6%
where the time goes in v1:
time: 513 us; the launch traced here: 506 us
  other arithmetic  262 us (51%)
  Pallas kernels  98.8 us (19%)
  matrix products  49.4 us (10%)
  local copies, waits for them, and re-layouts  39.2 us (8%)
  starting transfers between devices  38.8 us (8%)
  waiting for transfers between devices  9.57 us (2%)
  between operations  8.37 us (2%)
    another operation x21, other arithmetic, project_pencil(): lower = jnp.linalg.cholesky(normed_b)  113 us
    pallas_call x3, Pallas kernels, all_sum(): pl.pallas_call(functools.partial(sum_kernel, parts, axes, ncopies), out_s...  98.8 us
    another operation x5, other arithmetic, upper_solve(): lax.linalg.triangular_solve(lower, rhs, left_side=True, lower=True, trans...  60.1 us
    another operation x6, other arithmetic, project_pencil(): factor = jnp.linalg.cholesky(matmul(iterate.T, iterate))  25.7 us
    dot_general x31, matrix products, matmul(): jnp.dot(left, right, precision=lax.Precision.HIGHEST, preferred_element_t...  24.5 us
    another operation x4, other arithmetic, lower_solve(): return lax.linalg.triangular_solve(lower, rhs, left_side=True, lower=True)  23.4 us
    another operation x22, matrix products, lower_solve(): return lax.linalg.triangular_solve(lower, rhs, left_side=True, lower=True)  14.6 us
    ppermute x4, starting transfers between devices, extended_2(): lax.ppermute(lax.slice_in_dim(block, block.shape[dim] - width, None, axis...  13.9 us
  transfers between devices with their start and end apart: 12, of which 4 were waited for; matrix products, arithmetic and copies ran while one was open for 5% of the time, Pallas kernels for 6%

profile of v1, /device:TPU:1, one launch (start us, length us, event | category | flops | bytes accessed | tf_op | source)
XLA Modules:
  0.0 505.7 jit_solution(11011636589914564709)
XLA Ops:
  1.4 4.5 collective-permute-start
  7.6 4.1 all-to-all-start
  18.2 4.4 all-to-all-start.1
  22.8 3.5 collective-permute-start.1
  26.4 1.9 collective-permute-start.2
  29.3 3.1 collective-permute-start.5
  32.4 1.9 collective-permute-start.6
  34.4 2.3 select_maximum_fusion.6
  36.7 4.5 multiply_subtract_fusion.4
  41.7 28.5 %ritz_sum.1 = f32[128,128]{1,0:T(8,128)S(1)} custom-call(f32[128,128]{1,0:T(8,128)S(1)} %get-tuple-element.186.in_ref), custom_call_target="tpu_custom_call" | custom-call | tf_op jit(solution)/shard_map/ritz_sum/pallas_call | solution.py:163
  70.9 5.4 %collective-permute-start.3 = (f32[128,1,2,256]{3,2,0,1:T(2,128)S(1)}, f32[128,1,2,256]{3,2,0,1:T(2,128)S(1)}, u32[]{:S(2)}, u32[]{:S(2)}) collective-permute-start(f32[128,1,2,256]{3,2,0,1:T(2,128)S(1)} %reshape.233), channel_id=1, source_target_pairs={{0,1},{1,2},{2,3},{3,4},{4,5},{5,6},{6,7},{7,8},{8,9},{9,10},{10,1... | collective-permute-start | bytes 786440 | tf_op jit(solution)/shard_map/ppermute | solution.py:197
  76.3 2.2 collective-permute-start.4
  78.5 2.3 select_maximum_fusion.2
  80.8 4.4 fusion.83
  86.8 2.3 select_maximum_fusion.4
  89.3 4.4 fusion.108
  96.0 34.2 %gram_sum.2 = f32[1536,128]{1,0:T(8,128)S(1)} custom-call(f32[1536,128]{1,0:T(8,128)S(1)} %slice_dynamic-update-slice_fusion.10.in_ref), custom_call_target="tpu_custom_call" | custom-call | tf_op jit(solution)/shard_map/gram_sum/pallas_call | solution.py:163
  137.8 5.0 gather_fusion
  143.5 2.0 multiply_multiply_fusion.3
  146.6 11.7 %cholesky.250 = f32[128,128]{1,0:T(8,128)S(1)} custom-call(f32[128,128]{1,0:T(8,128)S(1)} %cholesky.374), custom_call_target="Cholesky" | custom-call | tf_op jit(solution)/shard_map/jit(cholesky)/cholesky | solution.py:226
  158.4 9.8 %custom-call.36 = f32[1,128,128]{1,2,0:T(8,128)S(1)} custom-call(f32[1,128,128]{2,1,0:T(8,128)S(1)} %get-tuple-element.146), custom_call_target="InvertDiagBlocksLowerTriangular" | custom-call | tf_op jit(solution)/shard_map/jit(cholesky)/cholesky | solution.py:226
  170.6 11.7 %cholesky.269 = f32[128,128]{1,0:T(8,128)S(1)} custom-call(f32[128,128]{1,0:T(8,128)S(1)} %cholesky.378), custom_call_target="Cholesky" | custom-call | tf_op jit(solution)/shard_map/jit(cholesky)/cholesky | solution.py:226
  182.4 9.9 %custom-call.37 = f32[1,128,128]{1,2,0:T(8,128)S(1)} custom-call(f32[1,128,128]{2,1,0:T(8,128)S(1)} %get-tuple-element.143), custom_call_target="InvertDiagBlocksLowerTriangular" | custom-call | tf_op jit(solution)/shard_map/jit(cholesky)/cholesky | solution.py:226
  193.7 11.7 %cholesky.288 = f32[128,128]{1,0:T(8,128)S(1)} custom-call(f32[128,128]{1,0:T(8,128)S(1)} %convolution_subtract_fusion.17), custom_call_target="Cholesky" | custom-call | tf_op jit(solution)/shard_map/jit(cholesky)/cholesky | solution.py:226
  208.7 6.0 %while.12 = (s32[]{:T(128)}, f32[384,384]{1,0:T(8,128)S(1)}, s32[3,2]{0,1:T(2,128)S(1)}, f32[3,128,128]{2,1,0:T(8,128)S(1)}, s32[]{:T(128)}) while((s32[]{:T(128)}, f32[384,384]{1,0:T(8,128)S(1)}, s32[3,2]{0,1:T(2,128)S(1)}, f32[3,128,128]{2,1,0:T(8,128)S(1)}, s32[]{:T(128)}) %tuple.152), condition=%wide.while_cond.1, body=%wide.while_body.1.sunk | while | flops 2 | bytes 131181 | solution.py:214
  214.7 29.7 %custom-call.41 = f32[3,128,128]{1,2,0:T(8,128)S(1)} custom-call(f32[3,128,128]{2,1,0:T(8,128)S(1)} %get-tuple-element.49), custom_call_target="InvertDiagBlocksLowerTriangular" | custom-call | tf_op jit(solution)/shard_map/triangular_solve/custom-call.8 | solution.py:214
  261.9 12.5 %cholesky.301 = f32[128,128]{1,0:T(8,128)S(1)} custom-call(f32[128,128]{1,0:T(8,128)} %fusion.224), custom_call_target="Cholesky" | custom-call | tf_op jit(solution)/shard_map/jit(cholesky)/cholesky | solution.py:233
  276.6 11.1 %custom-call.40 = f32[1,128,128]{1,2,0:T(8,128)S(1)} custom-call(f32[1,128,128]{2,1,0:T(8,128)} %fusion.204), custom_call_target="InvertDiagBlocksLowerTriangular" | custom-call | tf_op jit(solution)/shard_map/triangular_solve/custom-call.7 | solution.py:210
  291.5 2.0 fusion.17
  297.2 1.9 collective-permute-start.7
  299.1 2.4 collective-permute-start.8
  303.5 3.3 collective-permute-done.8
  306.8 2.3 select_maximum_fusion
  309.4 4.4 fusion.58
  315.9 36.1 %gram_sum.3 = f32[1536,128]{1,0:T(8,128)S(1)} custom-call(f32[1536,128]{1,0:T(8,128)S(1)} %slice_dynamic-update-slice_fusion.in_ref), custom_call_target="tpu_custom_call" | custom-call | tf_op jit(solution)/shard_map/gram_sum/pallas_call | solution.py:163
  353.5 3.6 gather_fusion.1
  358.5 11.7 %cholesky.314 = f32[128,128]{1,0:T(8,128)S(1)} custom-call(f32[128,128]{1,0:T(8,128)S(1)} %cholesky.382), custom_call_target="Cholesky" | custom-call | tf_op jit(solution)/shard_map/jit(cholesky)/cholesky | solution.py:226
  370.3 9.8 %custom-call.42 = f32[1,128,128]{1,2,0:T(8,128)S(1)} custom-call(f32[1,128,128]{2,1,0:T(8,128)S(1)} %get-tuple-element.139), custom_call_target="InvertDiagBlocksLowerTriangular" | custom-call | tf_op jit(solution)/shard_map/jit(cholesky)/cholesky | solution.py:226
  382.5 11.7 %cholesky.333 = f32[128,128]{1,0:T(8,128)S(1)} custom-call(f32[128,128]{1,0:T(8,128)S(1)} %cholesky.386), custom_call_target="Cholesky" | custom-call | tf_op jit(solution)/shard_map/jit(cholesky)/cholesky | solution.py:226
  395.5 10.0 %custom-call.43 = f32[1,128,128]{1,2,0:T(8,128)S(1)} custom-call(f32[1,128,128]{2,1,0:T(8,128)S(1)} %get-tuple-element.136), custom_call_target="InvertDiagBlocksLowerTriangular" | custom-call | tf_op jit(solution)/shard_map/jit(cholesky)/cholesky | solution.py:226
  406.8 11.7 %cholesky.352 = f32[128,128]{1,0:T(8,128)S(1)} custom-call(f32[128,128]{1,0:T(8,128)S(1)} %convolution_subtract_fusion.14), custom_call_target="Cholesky" | custom-call | tf_op jit(solution)/shard_map/jit(cholesky)/cholesky | solution.py:226
  421.2 6.2 %while.13 = (s32[]{:T(128)}, f32[384,384]{1,0:T(8,128)S(1)}, s32[3,2]{0,1:T(2,128)S(1)}, f32[3,128,128]{2,1,0:T(8,128)S(1)}, s32[]{:T(128)}) while((s32[]{:T(128)}, f32[384,384]{1,0:T(8,128)S(1)}, s32[3,2]{0,1:T(2,128)S(1)}, f32[3,128,128]{2,1,0:T(8,128)S(1)}, s32[]{:T(128)}) %tuple.158), condition=%wide.while_cond.1.clone, body=%wide.while_body.1.clone.sunk | while | flops 2 | bytes 131181 | solution.py:214
  427.5 29.7 %custom-call.47 = f32[3,128,128]{1,2,0:T(8,128)S(1)} custom-call(f32[3,128,128]{2,1,0:T(8,128)S(1)} %get-tuple-element.52), custom_call_target="InvertDiagBlocksLowerTriangular" | custom-call | tf_op jit(solution)/shard_map/triangular_solve/custom-call.8 | solution.py:214
  466.1 11.7 %cholesky.365 = f32[128,128]{1,0:T(8,128)S(1)} custom-call(f32[128,128]{1,0:T(8,128)S(1)} %fusion.218), custom_call_target="Cholesky" | custom-call | tf_op jit(solution)/shard_map/jit(cholesky)/cholesky | solution.py:233
  479.3 10.2 %custom-call.46 = f32[1,128,128]{1,2,0:T(8,128)S(1)} custom-call(f32[1,128,128]{2,1,0:T(8,128)S(1)} %fusion.205), custom_call_target="InvertDiagBlocksLowerTriangular" | custom-call | tf_op jit(solution)/shard_map/triangular_solve/custom-call.7 | solution.py:210
  491.4 2.1 fusion.15
  495.0 3.4 all-to-all-start.2
  499.7 5.2 %all-to-all-done.2 = f32[8,16,512]{2,1,0:T(8,128)S(1)} async-done(((f32[8,16,512]{2,1,0:T(8,128)}), f32[8,16,512]{2,1,0:T(8,128)S(1)}, u32[]{:S(2)}, u32[]{:S(2)}) %all-to-all-start.2) | async-done | bytes 262176 | tf_op jit(solution)/shard_map/all_to_all | solution.py:344
  (404 shorter events, 94.6 us)
Async XLA Ops:
  1.4 16.2 %collective-permute-start = (f32[13,1,2,256]{3,2,1,0:T(2,128)S(1)}, f32[13,1,2,256]{3,2,1,0:T(2,128)S(1)}, u32[]{:S(2)}, u32[]{:S(2)}) collective-permute-start(f32[13,1,2,256]{3,2,1,0:T(2,128)S(1)} %bitcast.385), channel_id=1, source_target_pairs={{0,1},{1,2},{2,3},{3,4},{4,5},{5,6},{6,7},{7,8},{8,9},{9,10},{10,1... | collective-permute-start | bytes 79880 | tf_op jit(solution)/shard_map/ppermute | solution.py:189
  7.6 10.6 %all-to-all-start = ((f32[16,8,512]{2,0,1:T(8,128)}), f32[16,8,512]{2,0,1:T(8,128)S(1)}, u32[]{:S(2)}, u32[]{:S(2)}) async-start(f32[16,8,512]{2,0,1:T(8,128)} %bitcast.332), calls=%async_computation | async-start | bytes 524288 | tf_op jit(solution)/shard_map/all_to_all | solution.py:320
  15.6 73.4 %copy-start.20 = (f32[2,256]{1,0:T(2,128)}, f32[2,256]{1,0:T(2,128)S(1)}, u32[]{:S(2)}) copy-start(f32[2,256]{1,0:T(2,128)S(1)} %mul.1073) | copy-start | bytes 6148
  15.7 73.4 %copy-start.22 = (f32[2,256]{1,0:T(2,128)}, f32[2,256]{1,0:T(2,128)S(1)}, u32[]{:S(2)}) copy-start(f32[2,256]{1,0:T(2,128)S(1)} %mul.1079) | copy-start | bytes 6148
  15.7 73.4 %copy-start.24 = (f32[2,256]{1,0:T(2,128)}, f32[2,256]{1,0:T(2,128)S(1)}, u32[]{:S(2)}) copy-start(f32[2,256]{1,0:T(2,128)S(1)} %mul.501) | copy-start | bytes 6148
  15.7 73.4 %copy-start.26 = (f32[2,256]{1,0:T(2,128)}, f32[2,256]{1,0:T(2,128)S(1)}, u32[]{:S(2)}) copy-start(f32[2,256]{1,0:T(2,128)S(1)} %mul.1037) | copy-start | bytes 6148
  15.7 73.4 %copy-start.28 = (f32[2,256]{1,0:T(2,128)}, f32[2,256]{1,0:T(2,128)S(1)}, u32[]{:S(2)}) copy-start(f32[2,256]{1,0:T(2,128)S(1)} %mul.1043) | copy-start | bytes 6148
  15.7 73.4 %copy-start.30 = (f32[2,256]{1,0:T(2,128)}, f32[2,256]{1,0:T(2,128)S(1)}, u32[]{:S(2)}) copy-start(f32[2,256]{1,0:T(2,128)S(1)} %mul.1049) | copy-start | bytes 6148
  15.8 73.4 %copy-start.32 = (f32[2,256]{1,0:T(2,128)}, f32[2,256]{1,0:T(2,128)S(1)}, u32[]{:S(2)}) copy-start(f32[2,256]{1,0:T(2,128)S(1)} %mul.1055) | copy-start | bytes 6148
  15.8 73.4 %copy-start.34 = (f32[2,256]{1,0:T(2,128)}, f32[2,256]{1,0:T(2,128)S(1)}, u32[]{:S(2)}) copy-start(f32[2,256]{1,0:T(2,128)S(1)} %mul.1085) | copy-start | bytes 6148
  15.8 73.4 %copy-start.36 = (f32[2,256]{1,0:T(2,128)}, f32[2,256]{1,0:T(2,128)S(1)}, u32[]{:S(2)}) copy-start(f32[2,256]{1,0:T(2,128)S(1)} %mul.1091) | copy-start | bytes 6148
  15.8 73.4 %copy-start.38 = (f32[2,256]{1,0:T(2,128)}, f32[2,256]{1,0:T(2,128)S(1)}, u32[]{:S(2)}) copy-start(f32[2,256]{1,0:T(2,128)S(1)} %mul.507) | copy-start | bytes 6148
  15.9 73.3 %copy-start.40 = (f32[2,256]{1,0:T(2,128)}, f32[2,256]{1,0:T(2,128)S(1)}, u32[]{:S(2)}) copy-start(f32[2,256]{1,0:T(2,128)S(1)} %mul.513) | copy-start | bytes 6148
  17.7 71.5 %copy-start.42 = (f32[2,256]{1,0:T(2,128)}, f32[2,256]{1,0:T(2,128)S(1)}, u32[]{:S(2)}) copy-start(f32[2,256]{1,0:T(2,128)S(1)} %slice_bitcast_fusion.24) | copy-start | bytes 6148
  18.2 10.9 %all-to-all-start.1 = ((f32[16,8,512]{2,0,1:T(8,128)}), f32[16,8,512]{2,0,1:T(8,128)S(1)}, u32[]{:S(2)}, u32[]{:S(2)}) async-start(f32[16,8,512]{2,0,1:T(8,128)} %bitcast.331), calls=%async_computation.1 | async-start | bytes 524288 | tf_op jit(solution)/shard_map/all_to_all | solution.py:321
  22.8 11.6 %collective-permute-start.1 = (f32[128,1,2,256]{3,2,0,1:T(2,128)S(1)}, f32[128,1,2,256]{3,2,0,1:T(2,128)S(1)}, u32[]{:S(2)}, u32[]{:S(2)}) collective-permute-start(f32[128,1,2,256]{3,2,0,1:T(2,128)S(1)} %all_to_all.47), channel_id=1, source_target_pairs={{0,1},{1,2},{2,3},{3,4},{4,5},{5,6},{6,7},{7,8},{8,9},{9,10},{10,1... | collective-permute-start | bytes 786440 | tf_op jit(solution)/shard_map/ppermute | solution.py:197
  26.4 8.0 %collective-permute-start.2 = (f32[128,1,2,256]{3,2,0,1:T(2,128)S(1)}, f32[128,1,2,256]{3,2,0,1:T(2,128)S(1)}, u32[]{:S(2)}, u32[]{:S(2)}) collective-permute-start(f32[128,1,2,256]{3,2,0,1:T(2,128)S(1)} %all_to_all.47), channel_id=1, source_target_pairs={{1,0},{2,1},{3,2},{4,3},{5,4},{6,5},{7,6},{8,7},{9,8},{10,9},{11,1... | collective-permute-start | bytes 786440 | tf_op jit(solution)/shard_map/ppermute | solution.py:200
  28.4 60.8 %copy-start.44 = (f32[2,256]{1,0:T(2,128)}, f32[2,256]{1,0:T(2,128)S(1)}, u32[]{:S(2)}) copy-start(f32[2,256]{1,0:T(2,128)S(1)} %get-tuple-element.121) | copy-start | bytes 6148
  28.4 60.8 %copy-start.46 = (f32[2,256]{1,0:T(2,128)}, f32[2,256]{1,0:T(2,128)S(1)}, u32[]{:S(2)}) copy-start(f32[2,256]{1,0:T(2,128)S(1)} %get-tuple-element.122) | copy-start | bytes 6148
  28.4 60.8 %copy-start.48 = (f32[2,256]{1,0:T(2,128)}, f32[2,256]{1,0:T(2,128)S(1)}, u32[]{:S(2)}) copy-start(f32[2,256]{1,0:T(2,128)S(1)} %get-tuple-element.123) | copy-start | bytes 6148
  28.4 60.8 %copy-start.50 = (f32[2,256]{1,0:T(2,128)}, f32[2,256]{1,0:T(2,128)S(1)}, u32[]{:S(2)}) copy-start(f32[2,256]{1,0:T(2,128)S(1)} %get-tuple-element.124) | copy-start | bytes 6148
  28.4 60.8 %copy-start.52 = (f32[2,256]{1,0:T(2,128)}, f32[2,256]{1,0:T(2,128)S(1)}, u32[]{:S(2)}) copy-start(f32[2,256]{1,0:T(2,128)S(1)} %get-tuple-element.125) | copy-start | bytes 6148
  28.4 60.8 %copy-start.54 = (f32[2,256]{1,0:T(2,128)}, f32[2,256]{1,0:T(2,128)S(1)}, u32[]{:S(2)}) copy-start(f32[2,256]{1,0:T(2,128)S(1)} %get-tuple-element.126) | copy-start | bytes 6148
  28.4 60.8 %copy-start.56 = (f32[2,256]{1,0:T(2,128)}, f32[2,256]{1,0:T(2,128)S(1)}, u32[]{:S(2)}) copy-start(f32[2,256]{1,0:T(2,128)S(1)} %get-tuple-element.127) | copy-start | bytes 6148
  28.4 60.8 %copy-start.58 = (f32[2,256]{1,0:T(2,128)}, f32[2,256]{1,0:T(2,128)S(1)}, u32[]{:S(2)}) copy-start(f32[2,256]{1,0:T(2,128)S(1)} %get-tuple-element.128) | copy-start | bytes 6148
  28.5 60.8 %copy-start.60 = (f32[2,256]{1,0:T(2,128)}, f32[2,256]{1,0:T(2,128)S(1)}, u32[]{:S(2)}) copy-start(f32[2,256]{1,0:T(2,128)S(1)} %get-tuple-element.129) | copy-start | bytes 6148
  28.5 60.8 %copy-start.62 = (f32[2,256]{1,0:T(2,128)}, f32[2,256]{1,0:T(2,128)S(1)}, u32[]{:S(2)}) copy-start(f32[2,256]{1,0:T(2,128)S(1)} %get-tuple-element.130) | copy-start | bytes 6148
  28.5 60.8 %copy-start.64 = (f32[2,256]{1,0:T(2,128)}, f32[2,256]{1,0:T(2,128)S(1)}, u32[]{:S(2)}) copy-start(f32[2,256]{1,0:T(2,128)S(1)} %get-tuple-element.131) | copy-start | bytes 6148
  28.5 60.8 %copy-start.66 = (f32[2,256]{1,0:T(2,128)}, f32[2,256]{1,0:T(2,128)S(1)}, u32[]{:S(2)}) copy-start(f32[2,256]{1,0:T(2,128)S(1)} %get-tuple-element.132) | copy-start | bytes 6148
  28.5 41.8 %copy-start.71 = (f32[512]{0:T(512)}, f32[512]{0:T(512)S(1)}, u32[]{:S(2)}) copy-start(f32[512]{0:T(512)S(1)} %get-tuple-element.183) | copy-start | bytes 6148
  28.5 65.3 %copy-start.69 = (f32[512]{0:T(512)}, f32[512]{0:T(512)S(1)}, u32[]{:S(2)}) copy-start(f32[512]{0:T(512)S(1)} %get-tuple-element.184) | copy-start | bytes 6148
  29.3 49.1 %collective-permute-start.5 = (f32[128,1,2,256]{3,2,0,1:T(2,128)S(1)}, f32[128,1,2,256]{3,2,0,1:T(2,128)S(1)}, u32[]{:S(2)}, u32[]{:S(2)}) collective-permute-start(f32[128,1,2,256]{3,2,0,1:T(2,128)S(1)} %reshape.235), channel_id=1, source_target_pairs={{0,1},{1,2},{2,3},{3,4},{4,5},{5,6},{6,7},{7,8},{8,9},{9,10},{10,1... | collective-permute-start | bytes 786440 | tf_op jit(solution)/shard_map/ppermute | solution.py:197
  32.4 46.0 %collective-permute-start.6 = (f32[128,1,2,256]{3,2,0,1:T(2,128)S(1)}, f32[128,1,2,256]{3,2,0,1:T(2,128)S(1)}, u32[]{:S(2)}, u32[]{:S(2)}) collective-permute-start(f32[128,1,2,256]{3,2,0,1:T(2,128)S(1)} %reshape.235), channel_id=1, source_target_pairs={{1,0},{2,1},{3,2},{4,3},{5,4},{6,5},{7,6},{8,7},{9,8},{10,9},{11,1... | collective-permute-start | bytes 786440 | tf_op jit(solution)/shard_map/ppermute | solution.py:200
  70.9 15.9 %collective-permute-start.3 = (f32[128,1,2,256]{3,2,0,1:T(2,128)S(1)}, f32[128,1,2,256]{3,2,0,1:T(2,128)S(1)}, u32[]{:S(2)}, u32[]{:S(2)}) collective-permute-start(f32[128,1,2,256]{3,2,0,1:T(2,128)S(1)} %reshape.233), channel_id=1, source_target_pairs={{0,1},{1,2},{2,3},{3,4},{4,5},{5,6},{6,7},{7,8},{8,9},{9,10},{10,1... | collective-permute-start | bytes 786440 | tf_op jit(solution)/shard_map/ppermute | solution.py:197
  76.3 10.5 %collective-permute-start.4 = (f32[128,1,2,256]{3,2,0,1:T(2,128)S(1)}, f32[128,1,2,256]{3,2,0,1:T(2,128)S(1)}, u32[]{:S(2)}, u32[]{:S(2)}) collective-permute-start(f32[128,1,2,256]{3,2,0,1:T(2,128)S(1)} %reshape.233), channel_id=1, source_target_pairs={{1,0},{2,1},{3,2},{4,3},{5,4},{6,5},{7,6},{8,7},{9,8},{10,9},{11,1... | collective-permute-start | bytes 786440 | tf_op jit(solution)/shard_map/ppermute | solution.py:200
  131.0 12.5 %copy-start.12 = (f32[128,128]{1,0:T(8,128)}, f32[128,128]{1,0:T(8,128)S(1)}, u32[]{:S(2)}) copy-start(f32[128,128]{1,0:T(8,128)S(1)} %get-tuple-element.115) | copy-start | bytes 196612
  131.0 12.5 %copy-start.14 = (f32[128,128]{1,0:T(8,128)}, f32[128,128]{1,0:T(8,128)S(1)}, u32[]{:S(2)}) copy-start(f32[128,128]{1,0:T(8,128)S(1)} %get-tuple-element.116) | copy-start | bytes 196612
  131.7 11.7 %copy-start = (f32[384,384]{0,1:T(8,128)}, f32[384,384]{0,1:T(8,128)S(1)}, u32[]{:S(2)}) copy-start(f32[384,384]{0,1:T(8,128)S(1)} %copy.91) | copy-start | bytes 1769476
  146.6 62.0 %copy-start.73 = (s32[3]{0:T(128)S(1)}, s32[3]{0:T(128)}, u32[]{:S(2)}) copy-start(s32[3]{0:T(128)} %iota_multiply_fusion) | copy-start | bytes 40
  256.8 34.6 %copy-start.1 = (f32[384,384]{0,1:T(8,128)S(1)}, f32[384,384]{0,1:T(8,128)}, u32[]{:S(2)}) copy-start(f32[384,384]{0,1:T(8,128)} %copy-done) | copy-start | bytes 1769476
  259.2 32.2 %copy-start.13 = (f32[128,128]{1,0:T(8,128)S(1)}, f32[128,128]{1,0:T(8,128)}, u32[]{:S(2)}) copy-start(f32[128,128]{1,0:T(8,128)} %copy-done.12) | copy-start | bytes 196612
  259.2 32.2 %copy-start.15 = (f32[128,128]{1,0:T(8,128)S(1)}, f32[128,128]{1,0:T(8,128)}, u32[]{:S(2)}) copy-start(f32[128,128]{1,0:T(8,128)} %copy-done.14) | copy-start | bytes 196612
  295.3 19.2 %copy-start.6 = (f32[128,512]{1,0:T(8,128)}, f32[128,512]{1,0:T(8,128)S(1)}, u32[]{:S(2)}) copy-start(f32[128,512]{1,0:T(8,128)S(1)} %fusion.32) | copy-start | bytes 786436
  297.2 6.3 %collective-permute-start.7 = (f32[128,1,2,256]{3,2,0,1:T(2,128)S(1)}, f32[128,1,2,256]{3,2,0,1:T(2,128)S(1)}, u32[]{:S(2)}, u32[]{:S(2)}) collective-permute-start(f32[128,1,2,256]{3,2,0,1:T(2,128)S(1)} %reshape.237), channel_id=1, source_target_pairs={{0,1},{1,2},{2,3},{3,4},{4,5},{5,6},{6,7},{7,8},{8,9},{9,10},{10,1... | collective-permute-start | bytes 786440 | tf_op jit(solution)/shard_map/ppermute | solution.py:197
  299.1 7.7 %collective-permute-start.8 = (f32[128,1,2,256]{3,2,0,1:T(2,128)S(1)}, f32[128,1,2,256]{3,2,0,1:T(2,128)S(1)}, u32[]{:S(2)}, u32[]{:S(2)}) collective-permute-start(f32[128,1,2,256]{3,2,0,1:T(2,128)S(1)} %reshape.237), channel_id=1, source_target_pairs={{1,0},{2,1},{3,2},{4,3},{5,4},{6,5},{7,6},{8,7},{9,8},{10,9},{11,1... | collective-permute-start | bytes 786440 | tf_op jit(solution)/shard_map/ppermute | solution.py:200
  465.5 25.9 %copy-start.17 = (f32[128,128]{1,0:T(8,128)S(1)}, f32[128,128]{1,0:T(8,128)}, u32[]{:S(2)}) copy-start(f32[128,128]{1,0:T(8,128)} %copy-done.16) | copy-start | bytes 196612
  477.9 15.6 %copy-start.7 = (f32[128,512]{1,0:T(8,128)S(1)}, f32[128,512]{1,0:T(8,128)}, u32[]{:S(2)}) copy-start(f32[128,512]{1,0:T(8,128)} %copy-done.6) | copy-start | bytes 786436
  495.0 9.9 %all-to-all-start.2 = ((f32[8,16,512]{2,1,0:T(8,128)}), f32[8,16,512]{2,1,0:T(8,128)S(1)}, u32[]{:S(2)}, u32[]{:S(2)}) async-start(f32[8,16,512]{2,1,0:T(8,128)} %bitcast.85), calls=%async_computation.2 | async-start | bytes 524288 | tf_op jit(solution)/shard_map/all_to_all | solution.py:344
  (38 other events, 200.2 us)

commit v2 on v1

--- a/solution.py
+++ b/solution.py
@@ -206,34 +206,146 @@
     return jnp.dot(left, right, precision=lax.Precision.HIGHEST, preferred_element_type=jnp.float32)
 
 
-def lower_solve(lower, rhs):
-    return lax.linalg.triangular_solve(lower, rhs, left_side=True, lower=True)
-
-
-def upper_solve(lower, rhs):
-    return lax.linalg.triangular_solve(lower, rhs, left_side=True, lower=True, transpose_a=True)
-
-
 def symmetric(matrix):
     return 0.5 * (matrix + matrix.T)
 
 
-def project_pencil(gram_a, gram_b, count):
-    sym_a = symmetric(gram_a)
-    scales = lax.rsqrt(jnp.diagonal(gram_b) + 1e-06)
-    normed_b = scales[:, None] * gram_b * scales[None, :]
-    normed_a = scales[:, None] * sym_a * scales[None, :]
-    lower = jnp.linalg.cholesky(normed_b)
-    half_way = lower_solve(lower, normed_a)
-    reduced = lower_solve(lower, half_way.T)
-    shift = 2.0 * jnp.max(jnp.sum(jnp.abs(reduced), axis=1))
-    iterate = jnp.eye(gram_a.shape[0], count, dtype=jnp.float32)
-    for sweep_index in range(QSTEPS):
-        iterate = iterate - matmul(reduced, iterate) / shift
-    factor = jnp.linalg.cholesky(matmul(iterate.T, iterate))
-    iterate = lower_solve(factor, iterate.T).T
-    coeffs = scales[:, None] * upper_solve(lower, iterate)
-    return coeffs, symmetric(matmul(coeffs.T, matmul(sym_a, coeffs)))
+def product(left, right, over=(1, 0)):
+    return lax.dot_general(
+        left, right, (((over[0],), (over[1],)), ((), ())),
+        precision=lax.Precision.HIGHEST, preferred_element_type=jnp.float32,
+    )
+
+
+SETTLED = 2e-3
+MOST_STEPS = 10
+
+
+def inverse_factor(matrix, step_ref, work_ref):
+    n = matrix.shape[0]
+    row = lax.broadcasted_iota(jnp.int32, (n, n), 0)
+    col = lax.broadcasted_iota(jnp.int32, (n, n), 1)
+    same = row == col
+    unit = jnp.where(same, 1.0, 0.0)
+    diag = jnp.where(same, matrix, 0.0)
+    scale_row = lax.rsqrt(jnp.sum(diag, axis=0, keepdims=True))
+    scale_col = lax.rsqrt(jnp.sum(diag, axis=1, keepdims=True))
+    scaled = scale_col * matrix * scale_row
+
+    def half(error):
+        return jnp.where(row > col, error, jnp.where(same, 0.5 * error, 0.0))
+
+    start = scaled - unit
+    step_ref[...] = unit - half(start)
+
+    def going(carry):
+        count, size = carry
+        return jnp.logical_and(count < MOST_STEPS, jnp.logical_not(size < SETTLED * SETTLED))
+
+    def step(carry):
+        count, _ = carry
+        now = step_ref[...]
+        error = product(product(now, scaled), now, (1, 1)) - unit
+        step_ref[...] = now - product(half(error), now)
+        return count + 1, jnp.sum(error * error)
+
+    _, size = lax.while_loop(going, step, (jnp.int32(0), jnp.sum(start * start)))
+
+    @pl.when(jnp.logical_not(size < SETTLED * SETTLED))
+    def _():
+        work_ref[...] = scaled
+        step_ref[...] = unit
+
+        def eliminate(j, carry):
+            work, done = work_ref[...], step_ref[...]
+            pivot_row = jnp.sum(jnp.where(row == j, work, 0.0), axis=0, keepdims=True)
+            pivot_col = jnp.sum(jnp.where(col == j, work, 0.0), axis=1, keepdims=True)
+            done_row = jnp.sum(jnp.where(row == j, done, 0.0), axis=0, keepdims=True)
+            pivot = jnp.sum(jnp.where(same & (row == j), work, 0.0))
+            factor = jnp.where(row > j, pivot_col / pivot, 0.0)
+            work_ref[...] = work - factor * pivot_row
+            done = done - factor * done_row
+            step_ref[...] = jnp.where(row == j, done * lax.rsqrt(jnp.full((1, n), pivot)), done)
+            return carry
+
+        lax.fori_loop(0, n, eliminate, 0)
+
+    return step_ref[...] * scale_row
+
+
+def pencil_kernel(sum_ref, coeff_ref, ritz_ref, image_ref, inverse_ref, step_ref, work_ref):
+    n = 128
+
+    def block(k):
+        return sum_ref[n * k:n * (k + 1)]
+
+    row = lax.broadcasted_iota(jnp.int32, (n, n), 0)
+    col = lax.broadcasted_iota(jnp.int32, (n, n), 1)
+    same = row == col
+    place = [(0, 0), (1, 0), (1, 1), (2, 0), (2, 1), (2, 2)]
+    across, down = [], []
+    for k in (6, 8, 11):
+        diag = jnp.where(same, block(k), 0.0)
+        across.append(lax.rsqrt(jnp.sum(diag, axis=0, keepdims=True) + 1e-06))
+        down.append(lax.rsqrt(jnp.sum(diag, axis=1, keepdims=True) + 1e-06))
+    normed = {}
+    for k, (i, j) in enumerate(place):
+        image = block(k)
+        field = block(6 + k)
+        if i == j:
+            image = 0.5 * (image + image.T)
+            field = 0.5 * (field + field.T)
+        image_ref[n * i:n * (i + 1), n * j:n * (j + 1)] = image
+        if i != j:
+            image_ref[n * j:n * (j + 1), n * i:n * (i + 1)] = image.T
+        normed[i, j] = down[i] * field * across[j]
+
+    inverse_0 = inverse_factor(normed[0, 0], step_ref, work_ref)
+    lower_10 = product(normed[1, 0], inverse_0, (1, 1))
+    lower_20 = product(normed[2, 0], inverse_0, (1, 1))
+    inverse_1 = inverse_factor(normed[1, 1] - product(lower_10, lower_10, (1, 1)), step_ref, work_ref)
+    lower_21 = product(normed[2, 1] - product(lower_20, lower_10, (1, 1)), inverse_1, (1, 1))
+    rest = normed[2, 2] - product(lower_20, lower_20, (1, 1)) - product(lower_21, lower_21, (1, 1))
+    inverse_10 = -product(inverse_1, product(lower_10, inverse_0))
+    inner_20 = product(lower_20, inverse_0) + product(lower_21, inverse_10)
+    inner_21 = product(lower_21, inverse_1)
+    inverse_2 = inverse_factor(rest, step_ref, work_ref)
+    inverse_ref[...] = jnp.zeros((3 * n, 3 * n), jnp.float32)
+    inverse_ref[0:n, 0:n] = inverse_0 * across[0]
+    inverse_ref[n:2 * n, 0:n] = inverse_10 * across[0]
+    inverse_ref[n:2 * n, n:2 * n] = inverse_1 * across[1]
+    inverse_ref[2 * n:, 0:n] = -product(inverse_2, inner_20) * across[0]
+    inverse_ref[2 * n:, n:2 * n] = -product(inverse_2, inner_21) * across[1]
+    inverse_ref[2 * n:, 2 * n:] = inverse_2 * across[2]
+    reduced = product(product(inverse_ref[...], image_ref[...]), inverse_ref[...], (1, 1))
+    shift = 2.0 * jnp.max(jnp.sum(jnp.abs(reduced), axis=1, keepdims=True))
+    reduced = reduced * (1.0 / jnp.full((1, 3 * n), shift))
+    tall_row = lax.broadcasted_iota(jnp.int32, (3 * n, n), 0)
+    tall_col = lax.broadcasted_iota(jnp.int32, (3 * n, n), 1)
+    iterate = jnp.where(tall_row == tall_col, 1.0, 0.0) - reduced[:, :n]
+    for _ in range(QSTEPS - 1):
+        iterate = iterate - product(reduced, iterate)
+    factor = inverse_factor(product(iterate, iterate, (0, 0)), step_ref, work_ref)
+    iterate = product(iterate, factor, (1, 1))
+    coeffs = product(inverse_ref[...], iterate, (0, 0))
+    coeff_ref[...] = coeffs
+    quotient = product(coeffs, product(image_ref[...], coeffs), (0, 0))
+    ritz_ref[...] = 0.5 * (quotient + quotient.T)
+
+
+def solve_pencil(summed):
+    n = 128
+    square = pltpu.VMEM((3 * n, 3 * n), jnp.float32)
+    small = pltpu.VMEM((n, n), jnp.float32)
+    return pl.pallas_call(
+        pencil_kernel,
+        out_shape=(jax.ShapeDtypeStruct((3 * n, n), jnp.float32), jax.ShapeDtypeStruct((n, n), jnp.float32)),
+        in_specs=[pl.BlockSpec(memory_space=pltpu.VMEM)],
+        out_specs=[pl.BlockSpec(memory_space=pltpu.VMEM)] * 2,
+        scratch_shapes=[square, square, small, small],
+        compiler_params=pltpu.CompilerParams(vmem_limit_bytes=32 << 20),
+        name="pencil",
+    )(summed)
 
 
 def neighbour_sum(padded, coupled):
@@ -283,11 +395,6 @@
     return jnp.concatenate([row[:, 128 * k:128 * (k + 1)] for row in rows for k in range(row.shape[1] // 128)])
 
 
-def unstacked(array):
-    b = [array[128 * k:128 * (k + 1)] for k in range(6)]
-    return jnp.block([[b[0], b[1].T, b[3].T], [b[1], b[2], b[4].T], [b[3], b[4], b[5]]])
-
-
 def on_device(start_modes, start_dirs, coupling, relax_class, relaxivity):
     local_voxels = coupling.shape[1]
     match = relax_class[:, None] == jnp.arange(relaxivity.shape[0], dtype=jnp.int32)[None, :]
@@ -334,7 +441,7 @@
         local_a = stacked(gram_blocks(fields, [images, search_images, dir_images]))
         local_b = stacked(gram_blocks(fields, fields))
         summed = all_sum(jnp.concatenate([local_a, local_b]), GRAM_LAYOUT, 2, "gram_sum")
-        coeffs, ritz = project_pencil(unstacked(summed[:768]), unstacked(summed[768:]), count)
+        coeffs, ritz = solve_pencil(summed)
         modes = matmul(coeffs.T, basis)
         images = matmul(coeffs.T, basis_images)
         dirs = matmul(coeffs[count:].T, basis[count:])

time: 513 us -> 322 us (0.63)
  other arithmetic: 262 us -> 29.2 us
  Pallas kernels: 98.8 us -> 216 us
  matrix products: 49.4 us -> 11.1 us
  local copies, waits for them, and re-layouts: 39.2 us -> 7.46 us
  blocking collectives: 0 us -> 9.26 us
  between operations: 8.37 us -> 1.51 us
    another operation x36 -> x0, other arithmetic: 222 us -> none  [the longest x21 113 us: project_pencil(): lower = jnp.linalg.cholesky(normed_b)]
    pallas_call x0 -> x2, Pallas kernels: none -> 118 us  [solve_pencil(): pl.pallas_call(pencil_kernel, out_shape=(jax.ShapeDtypeStruct((3 * n, n),...]
    another operation x40 -> x0, matrix products: 24.9 us -> none  [the longest x22 14.6 us: lower_solve(): return lax.linalg.triangular_solve(lower, rhs, left_side=True, lower=True)]
    dot_general x31 -> x19, matrix products: 24.5 us -> 11.1 us  [matmul(): jnp.dot(left, right, precision=lax.Precision.HIGHEST, preferred_element_t...]
    another operation x27 -> x0, local copies, waits for them, and re-layouts: 12.3 us -> none  [the longest x21 12.2 us: upper_solve(): lax.linalg.triangular_solve(lower, rhs, left_side=True, lower=True, trans...]
    all_to_all x0 -> x1, blocking collectives: none -> 9.26 us  [on_device(): lax.all_to_all(scaled, 'col', split_axis=0, concat_axis=1, tiled=True)]
    gather x2 -> x0, local copies, waits for them, and re-layouts: 8.64 us -> none  [project_pencil(): scales = lax.rsqrt(jnp.diagonal(gram_b) + 1e-06)]
    unnamed x184 -> x24, local copies, waits for them, and re-layouts: 6.93 us -> 0.22 us
  transfers between devices with their start and end apart: 12 -> 11, of which waited for: 4 -> 3; matrix products, arithmetic and copies ran while one was open for 5% -> 8% of each run, Pallas kernels for 6% -> 9%
where the time goes in v2:
time: 322 us; the launch traced here: 316 us
  Pallas kernels  216 us (67%)
  starting transfers between devices  35.7 us (11%)
  other arithmetic  29.2 us (9%)
  matrix products  11.1 us (3%)
  blocking collectives  9.26 us (3%)
  local copies, waits for them, and re-layouts  7.46 us (2%)
  waiting for transfers between devices  5.02 us (2%)
    pallas_call x2, Pallas kernels, solve_pencil(): pl.pallas_call(pencil_kernel, out_shape=(jax.ShapeDtypeStruct((3 * n, n),...  118 us
    pallas_call x3, Pallas kernels, all_sum(): pl.pallas_call(functools.partial(sum_kernel, parts, axes, ncopies), out_s...  98.7 us
    ppermute x4, starting transfers between devices, extended_2(): lax.ppermute(lax.slice_in_dim(block, block.shape[dim] - width, None, axis...  14 us
    add x3, other arithmetic, neighbour_sum(): total = total + back[None] * behind  13.2 us
    dot_general x19, matrix products, matmul(): jnp.dot(left, right, precision=lax.Precision.HIGHEST, preferred_element_t...  11.1 us
    all_to_all x1, blocking collectives, on_device(): lax.all_to_all(scaled, 'col', split_axis=0, concat_axis=1, tiled=True)  9.26 us
    concatenate x4, other arithmetic, extended_2(): block = jnp.concatenate([low, block, high], axis=dim)  9.19 us
    ppermute x4, starting transfers between devices, extended_2(): lax.ppermute(lax.slice_in_dim(block, 0, width, axis=dim), axis, backward)  8.76 us
  transfers between devices with their start and end apart: 11, of which 3 were waited for; matrix products, arithmetic and copies ran while one was open for 8% of the time, Pallas kernels for 9%

profile of v2, /device:TPU:1, one launch (start us, length us, event | category | flops | bytes accessed | tf_op | source)
XLA Modules:
  0.0 315.6 jit_solution(11124225665290713277)
XLA Ops:
  0.6 0.8 reshape.167
  1.4 4.5 %collective-permute-start = (f32[13,1,2,256]{3,2,1,0:T(2,128)S(1)}, f32[13,1,2,256]{3,2,1,0:T(2,128)S(1)}, u32[]{:S(2)}, u32[]{:S(2)}) collective-permute-start(f32[13,1,2,256]{3,2,1,0:T(2,128)S(1)} %bitcast.147), channel_id=1, source_target_pairs={{0,1},{1,2},{2,3},{3,4},{4,5},{5,6},{6,7},{7,8},{8,9},{9,10},{10,1... | collective-permute-start | bytes 79880 | tf_op jit(solution)/shard_map/ppermute | solution.py:189
  5.9 1.7 copy.31
  7.6 4.1 %all-to-all-start = ((f32[16,8,512]{2,0,1:T(8,128)}), f32[16,8,512]{2,0,1:T(8,128)S(1)}, u32[]{:S(2)}, u32[]{:S(2)}) async-start(f32[16,8,512]{2,0,1:T(8,128)} %bitcast.119), calls=%async_computation | async-start | bytes 524288 | tf_op jit(solution)/shard_map/all_to_all | solution.py:427
  11.7 1.0 fusion.219
  12.7 1.1 fusion.218
  14.1 0.8 select_reduce_fusion
  15.3 1.7 copy.30
  17.2 1.1 all-to-all-done
  18.3 4.4 %all-to-all-start.1 = ((f32[16,8,512]{2,0,1:T(8,128)}), f32[16,8,512]{2,0,1:T(8,128)S(1)}, u32[]{:S(2)}, u32[]{:S(2)}) async-start(f32[16,8,512]{2,0,1:T(8,128)} %bitcast.118), calls=%async_computation.1 | async-start | bytes 524288 | tf_op jit(solution)/shard_map/all_to_all | solution.py:428
  22.8 3.5 %collective-permute-start.1 = (f32[128,1,2,256]{3,2,0,1:T(2,128)S(1)}, f32[128,1,2,256]{3,2,0,1:T(2,128)S(1)}, u32[]{:S(2)}, u32[]{:S(2)}) collective-permute-start(f32[128,1,2,256]{3,2,0,1:T(2,128)S(1)} %all_to_all.47), channel_id=1, source_target_pairs={{0,1},{1,2},{2,3},{3,4},{4,5},{5,6},{6,7},{7,8},{8,9},{9,10},{10,1... | collective-permute-start | bytes 786440 | tf_op jit(solution)/shard_map/ppermute | solution.py:197
  26.3 1.9 collective-permute-start.2
  28.4 0.8 all-to-all-done.1
  29.3 3.1 collective-permute-start.5
  32.4 1.9 collective-permute-start.6
  34.4 2.3 select_maximum_fusion.6
  36.7 4.5 %multiply_subtract_fusion.4 = (f32[128,1,2,256]{3,2,0,1:T(2,128)S(1)}, f32[128,1,2,256]{3,2,0,1:T(2,128)S(1)}) fusion(f32[128,1,2,256]{3,2,0,1:T(2,128)S(1)} %all_to_all.47, f32[2,256]{1,0:T(2,128)S(1)} %get-tuple-element.26, f32[128,3,4,258]{3,2,0,1:T(4,128)S(1)} %select_maximum_fusion.6, f32[2,256]{1,0:T(2,128)S(1)} %get-tuple-element.39, ...), kind=kLoop, calls=%fused_computation.276 | loop fusion | flops 3473408 | bytes 7657472 | tf_op jit(solution)/shard_map/sub | solution.py:422
  41.7 28.4 %ritz_sum.1 = f32[128,128]{1,0:T(8,128)S(1)} custom-call(f32[128,128]{1,0:T(8,128)S(1)} %get-tuple-element.71.in_ref), custom_call_target="tpu_custom_call" | custom-call | tf_op jit(solution)/shard_map/ritz_sum/pallas_call | solution.py:163
  70.7 5.4 %collective-permute-start.3 = (f32[128,1,2,256]{3,2,0,1:T(2,128)S(1)}, f32[128,1,2,256]{3,2,0,1:T(2,128)S(1)}, u32[]{:S(2)}, u32[]{:S(2)}) collective-permute-start(f32[128,1,2,256]{3,2,0,1:T(2,128)S(1)} %reshape.171), channel_id=1, source_target_pairs={{0,1},{1,2},{2,3},{3,4},{4,5},{5,6},{6,7},{7,8},{8,9},{9,10},{10,1... | collective-permute-start | bytes 786440 | tf_op jit(solution)/shard_map/ppermute | solution.py:197
  76.1 2.1 collective-permute-start.4
  78.2 2.3 select_maximum_fusion.2
  80.5 4.4 %fusion.63 = f32[128,1,2,256]{3,2,0,1:T(2,128)S(1)} fusion(f32[128,3,4,258]{3,2,0,1:T(4,128)S(1)} %select_maximum_fusion.2, f32[128,1,2,256]{3,2,0,1:T(2,128)S(1)} %collective-permute-done.5, f32[128,1,2,256]{3,2,0,1:T(2,128)S(1)} %collective-permute-done.6, f32[2,256]{1,0:T(2,128)S(1)} %get-tuple-element.39, f32[2,256]{1,0:T(2,128)S(1)} %mul.994, ...), kind=kLoop, calls=%fused_computation.126 | loop fusion | flops 3342336 | bytes 7131136 | tf_op jit(solution)/shard_map/add | solution.py:377
  84.9 0.7 fusion.18
  85.6 0.8 convolution_bitcast_fusion
  86.5 2.3 select_maximum_fusion.4
  88.8 4.4 %fusion.88 = f32[128,1,2,256]{3,2,0,1:T(2,128)S(1)} fusion(f32[128,3,4,258]{3,2,0,1:T(4,128)S(1)} %select_maximum_fusion.4, f32[128,1,2,256]{3,2,0,1:T(2,128)S(1)} %collective-permute-done.3, f32[128,1,2,256]{3,2,0,1:T(2,128)S(1)} %collective-permute-done.4, f32[2,256]{1,0:T(2,128)S(1)} %get-tuple-element.39, f32[2,256]{1,0:T(2,128)S(1)} %mul.994, ...), kind=kLoop, calls=%fused_computation.175 | loop fusion | flops 3342336 | bytes 7131136 | tf_op jit(solution)/shard_map/add | solution.py:377
  93.3 0.7 fusion.14
  94.0 0.8 convolution_bitcast_fusion.1
  95.4 34.2 %gram_sum.2.sum_ref = f32[1536,128]{1,0:T(8,128)S(1)} custom-call(f32[1536,128]{1,0:T(8,128)S(1)} %slice_dynamic-update-slice_fusion.10.in_ref), custom_call_target="tpu_custom_call" | custom-call | tf_op jit(solution)/shard_map/gram_sum/pallas_call | solution.py:163
  129.6 98.5 %pencil.2 = (f32[384,128]{1,0:T(8,128)S(1)}, f32[128,128]{1,0:T(8,128)S(1)}) custom-call(f32[1536,128]{1,0:T(8,128)S(1)} %gram_sum.2.sum_ref), custom_call_target="tpu_custom_call" | custom-call | tf_op jit(solution)/shard_map/pencil/pallas_call | solution.py:340
  228.1 0.5 fusion.26
  228.5 0.7 fusion.13
  229.2 0.7 fusion.12
  230.2 0.7 fusion.34
  231.1 1.9 collective-permute-start.7
  233.0 2.8 collective-permute-start.8
  235.8 0.8 fusion.11
  236.7 0.5 fusion.30
  237.5 3.2 %collective-permute-done.8 = f32[128,1,2,256]{3,2,0,1:T(2,128)S(1)} collective-permute-done((f32[128,1,2,256]{3,2,0,1:T(2,128)S(1)}, f32[128,1,2,256]{3,2,0,1:T(2,128)S(1)}, u32[]{:S(2)}, u32[]{:S(2)}) %collective-permute-start.8) | collective-permute-done | bytes 262176 | tf_op jit(solution)/shard_map/ppermute | solution.py:200
  240.7 2.3 select_maximum_fusion
  243.0 4.4 %fusion.38 = f32[128,1,2,256]{3,2,0,1:T(2,128)S(1)} fusion(f32[128,3,4,258]{3,2,0,1:T(4,128)S(1)} %select_maximum_fusion, f32[128,1,2,256]{3,2,0,1:T(2,128)S(1)} %collective-permute-done.7, f32[128,1,2,256]{3,2,0,1:T(2,128)S(1)} %collective-permute-done.8, f32[2,256]{1,0:T(2,128)S(1)} %get-tuple-element.39, f32[2,256]{1,0:T(2,128)S(1)} %mul.994, ...), kind=kLoop, calls=%fused_computation.77 | loop fusion | flops 3342336 | bytes 7131136 | tf_op jit(solution)/shard_map/add | solution.py:377
  247.5 0.7 fusion.22
  248.2 0.8 fusion.5
  249.5 36.1 %gram_sum.3.sum_ref = f32[1536,128]{1,0:T(8,128)S(1)} custom-call(f32[1536,128]{1,0:T(8,128)S(1)} %slice_dynamic-update-slice_fusion.in_ref), custom_call_target="tpu_custom_call" | custom-call | tf_op jit(solution)/shard_map/gram_sum/pallas_call | solution.py:163
  285.6 19.1 %pencil.3 = (f32[384,128]{1,0:T(8,128)S(1)}, f32[128,128]{1,0:T(8,128)}) custom-call(f32[1536,128]{1,0:T(8,128)S(1)} %gram_sum.3.sum_ref), custom_call_target="tpu_custom_call" | custom-call | tf_op jit(solution)/shard_map/pencil/pallas_call | solution.py:340
  304.8 0.7 convolution_multiply_fusion
  305.4 9.3 %all_to_all.60 = f32[8,16,512]{2,1,0:T(8,128)S(1)} all-to-all(f32[8,16,512]{2,1,0:T(8,128)S(1)} %bitcast.137), channel_id=1, replica_groups=mesh['vox'=32,'col'=8] {'col'}, dimensions={0} | all-to-all | bytes 524288 | tf_op jit(solution)/shard_map/all_to_all | solution.py:451
  314.7 0.7 copy.21
  (85 shorter events, 4.5 us)
Async XLA Ops:
  1.4 15.5 %collective-permute-start = (f32[13,1,2,256]{3,2,1,0:T(2,128)S(1)}, f32[13,1,2,256]{3,2,1,0:T(2,128)S(1)}, u32[]{:S(2)}, u32[]{:S(2)}) collective-permute-start(f32[13,1,2,256]{3,2,1,0:T(2,128)S(1)} %bitcast.147), channel_id=1, source_target_pairs={{0,1},{1,2},{2,3},{3,4},{4,5},{5,6},{6,7},{7,8},{8,9},{9,10},{10,1... | collective-permute-start | bytes 79880 | tf_op jit(solution)/shard_map/ppermute | solution.py:189
  7.6 10.6 %all-to-all-start = ((f32[16,8,512]{2,0,1:T(8,128)}), f32[16,8,512]{2,0,1:T(8,128)S(1)}, u32[]{:S(2)}, u32[]{:S(2)}) async-start(f32[16,8,512]{2,0,1:T(8,128)} %bitcast.119), calls=%async_computation | async-start | bytes 524288 | tf_op jit(solution)/shard_map/all_to_all | solution.py:427
  18.3 10.9 %all-to-all-start.1 = ((f32[16,8,512]{2,0,1:T(8,128)}), f32[16,8,512]{2,0,1:T(8,128)S(1)}, u32[]{:S(2)}, u32[]{:S(2)}) async-start(f32[16,8,512]{2,0,1:T(8,128)} %bitcast.118), calls=%async_computation.1 | async-start | bytes 524288 | tf_op jit(solution)/shard_map/all_to_all | solution.py:428
  22.8 11.6 %collective-permute-start.1 = (f32[128,1,2,256]{3,2,0,1:T(2,128)S(1)}, f32[128,1,2,256]{3,2,0,1:T(2,128)S(1)}, u32[]{:S(2)}, u32[]{:S(2)}) collective-permute-start(f32[128,1,2,256]{3,2,0,1:T(2,128)S(1)} %all_to_all.47), channel_id=1, source_target_pairs={{0,1},{1,2},{2,3},{3,4},{4,5},{5,6},{6,7},{7,8},{8,9},{9,10},{10,1... | collective-permute-start | bytes 786440 | tf_op jit(solution)/shard_map/ppermute | solution.py:197
  26.3 8.1 %collective-permute-start.2 = (f32[128,1,2,256]{3,2,0,1:T(2,128)S(1)}, f32[128,1,2,256]{3,2,0,1:T(2,128)S(1)}, u32[]{:S(2)}, u32[]{:S(2)}) collective-permute-start(f32[128,1,2,256]{3,2,0,1:T(2,128)S(1)} %all_to_all.47), channel_id=1, source_target_pairs={{1,0},{2,1},{3,2},{4,3},{5,4},{6,5},{7,6},{8,7},{9,8},{10,9},{11,1... | collective-permute-start | bytes 786440 | tf_op jit(solution)/shard_map/ppermute | solution.py:200
  29.3 48.9 %collective-permute-start.5 = (f32[128,1,2,256]{3,2,0,1:T(2,128)S(1)}, f32[128,1,2,256]{3,2,0,1:T(2,128)S(1)}, u32[]{:S(2)}, u32[]{:S(2)}) collective-permute-start(f32[128,1,2,256]{3,2,0,1:T(2,128)S(1)} %reshape.173), channel_id=1, source_target_pairs={{0,1},{1,2},{2,3},{3,4},{4,5},{5,6},{6,7},{7,8},{8,9},{9,10},{10,1... | collective-permute-start | bytes 786440 | tf_op jit(solution)/shard_map/ppermute | solution.py:197
  32.4 45.8 %collective-permute-start.6 = (f32[128,1,2,256]{3,2,0,1:T(2,128)S(1)}, f32[128,1,2,256]{3,2,0,1:T(2,128)S(1)}, u32[]{:S(2)}, u32[]{:S(2)}) collective-permute-start(f32[128,1,2,256]{3,2,0,1:T(2,128)S(1)} %reshape.173), channel_id=1, source_target_pairs={{1,0},{2,1},{3,2},{4,3},{5,4},{6,5},{7,6},{8,7},{9,8},{10,9},{11,1... | collective-permute-start | bytes 786440 | tf_op jit(solution)/shard_map/ppermute | solution.py:200
  70.7 15.7 %collective-permute-start.3 = (f32[128,1,2,256]{3,2,0,1:T(2,128)S(1)}, f32[128,1,2,256]{3,2,0,1:T(2,128)S(1)}, u32[]{:S(2)}, u32[]{:S(2)}) collective-permute-start(f32[128,1,2,256]{3,2,0,1:T(2,128)S(1)} %reshape.171), channel_id=1, source_target_pairs={{0,1},{1,2},{2,3},{3,4},{4,5},{5,6},{6,7},{7,8},{8,9},{9,10},{10,1... | collective-permute-start | bytes 786440 | tf_op jit(solution)/shard_map/ppermute | solution.py:197
  76.1 10.4 %collective-permute-start.4 = (f32[128,1,2,256]{3,2,0,1:T(2,128)S(1)}, f32[128,1,2,256]{3,2,0,1:T(2,128)S(1)}, u32[]{:S(2)}, u32[]{:S(2)}) collective-permute-start(f32[128,1,2,256]{3,2,0,1:T(2,128)S(1)} %reshape.171), channel_id=1, source_target_pairs={{1,0},{2,1},{3,2},{4,3},{5,4},{6,5},{7,6},{8,7},{9,8},{10,9},{11,1... | collective-permute-start | bytes 786440 | tf_op jit(solution)/shard_map/ppermute | solution.py:200
  231.1 6.4 %collective-permute-start.7 = (f32[128,1,2,256]{3,2,0,1:T(2,128)S(1)}, f32[128,1,2,256]{3,2,0,1:T(2,128)S(1)}, u32[]{:S(2)}, u32[]{:S(2)}) collective-permute-start(f32[128,1,2,256]{3,2,0,1:T(2,128)S(1)} %reshape.175), channel_id=1, source_target_pairs={{0,1},{1,2},{2,3},{3,4},{4,5},{5,6},{6,7},{7,8},{8,9},{9,10},{10,1... | collective-permute-start | bytes 786440 | tf_op jit(solution)/shard_map/ppermute | solution.py:197
  233.0 7.7 %collective-permute-start.8 = (f32[128,1,2,256]{3,2,0,1:T(2,128)S(1)}, f32[128,1,2,256]{3,2,0,1:T(2,128)S(1)}, u32[]{:S(2)}, u32[]{:S(2)}) collective-permute-start(f32[128,1,2,256]{3,2,0,1:T(2,128)S(1)} %reshape.175), channel_id=1, source_target_pairs={{1,0},{2,1},{3,2},{4,3},{5,4},{6,5},{7,6},{8,7},{9,8},{10,9},{11,1... | collective-permute-start | bytes 786440 | tf_op jit(solution)/shard_map/ppermute | solution.py:200

commit v3 on v2

v3 whole, which is shorter than its diff:
```python
import functools
import math

import jax
import jax.numpy as jnp
from jax import lax
from jax.experimental import pallas as pl
from jax.experimental.pallas import tpu as pltpu
from jax.sharding import PartitionSpec as P

NX = 256
NZ = 2
HALF = 13
ITERS = 2
QSTEPS = 3


SIZES = {"core": 2, "x": 4, "y": 4, "z": 8}


def digit(axis):
    if axis in ("core", "x"):
        c = lax.axis_index("col")
        return lax.rem(c, 2) if axis == "core" else lax.div(c, 2)
    v = lax.axis_index("vox")
    return lax.rem(v, 4) if axis == "y" else lax.div(v, 4)


def peer(axis, step):
    size = SIZES[axis]
    other = lax.rem(digit(axis) + step, size)
    if axis == "core":
        return {"col": digit("x") * 2 + other}
    if axis == "x":
        return {"col": other * 2 + digit("core")}
    if axis == "y":
        return {"vox": digit("z") * 4 + other}
    return {"vox": other * 4 + digit("y")}


def beside(step):
    place = lax.rem(lax.axis_index("vox") * 8 + lax.axis_index("col") + step + 256, 256)
    return {"vox": lax.div(place, 8), "col": lax.rem(place, 8)}


def greet(axes):
    barrier = pltpu.get_barrier_semaphore()
    devices = [beside(1), beside(-1)]
    for axis in axes:
        devices += [peer(axis, step) for step in range(1, SIZES[axis])]
    for device in devices:
        pl.semaphore_signal(barrier, inc=1, device_id=device, device_id_type=pl.DeviceIdType.MESH)
    pl.semaphore_wait(barrier, len(devices))


class Copies:
    def __init__(self, send, recv):
        self.send, self.recv, self.all = send, recv, []

    def launch(self, src, dst, device):
        k = len(self.all)
        copy = pltpu.make_async_remote_copy(
            src_ref=src, dst_ref=dst, send_sem=self.send.at[k], recv_sem=self.recv.at[k],
            device_id=device, device_id_type=pl.DeviceIdType.MESH,
        )
        copy.start()
        self.all.append(copy)
        return copy

    def drain(self):
        for copy in self.all:
            copy.wait_send()


def plan(layout):
    rows, stages = layout
    scratch, steps, copies = [], [], 0
    for axis, kind in stages:
        size = SIZES[axis]
        if kind == "scatter":
            rows = rows // size
        scratch += [pltpu.VMEM((size, rows, 128), jnp.float32), pltpu.VMEM((rows, 128), jnp.float32)]
        steps.append((axis, kind, rows))
        copies += (size - 1) * (2 if kind == "scatter" else 1)
    return scratch, steps, copies


class Share:
    def __init__(self, layout, start, in_ref, out_ref, scratch, copies):
        _, self.steps, _ = plan(layout)
        self.gathers = [s for s in self.steps if s[1] == "scatter"][::-1]
        self.length = len(self.steps) + len(self.gathers)
        self.ref, self.at, self.start = in_ref, start, start
        self.out_ref, self.scratch, self.copies = out_ref, scratch, copies
        self.next = 0

    def begin(self):
        s = self.next
        self.waiting = []
        if s < len(self.steps):
            axis, kind, rows = self.steps[s]
            size = SIZES[axis]
            me = digit(axis)
            for step in range(1, size):
                if kind == "scatter":
                    at = self.at + lax.rem(me + step, size) * rows
                else:
                    at = self.at
                source = self.ref.at[pl.ds(pl.multiple_of(at, 8), rows)]
                self.waiting.append(self.copies.launch(source, self.scratch[2 * s].at[step], peer(axis, step)))
        elif s < self.length:
            axis, _, rows = self.gathers[s - len(self.steps)]
            mine = self.out_ref.at[pl.ds(pl.multiple_of(self.start, 8), rows)]
            self.waiting = [self.copies.launch(mine, mine, peer(axis, step)) for step in range(1, SIZES[axis])]

    def finish(self):
        s = self.next
        self.next += 1
        for copy in self.waiting:
            copy.wait_recv()
        if s < len(self.steps):
            axis, kind, rows = self.steps[s]
            size = SIZES[axis]
            me = digit(axis)
            landing = self.scratch[2 * s]
            if kind == "scatter":
                total = self.ref[pl.ds(pl.multiple_of(self.at + me * rows, 8), rows)]
                for step in range(1, size):
                    total = total + landing[step]
                self.start = self.start + me * rows
            else:
                landing[0] = self.ref[pl.ds(pl.multiple_of(self.at, 8), rows)]
                total = landing[me]
                for k in range(1, size):
                    total = total + landing[lax.rem(me - k + size, size)]
            if s == len(self.steps) - 1:
                self.out_ref[pl.ds(pl.multiple_of(self.start, 8), rows)] = total
            else:
                self.scratch[2 * s + 1][...] = total
                self.ref, self.at = self.scratch[2 * s + 1], 0
        elif s < self.length:
            axis, _, rows = self.gathers[s - len(self.steps)]
            self.start = self.start - digit(axis) * rows

    def turn(self):
        if self.next < self.length:
            self.finish()
            self.begin()


def through(shares):
    while any(s.next < s.length for s in shares):
        for share in shares:
            share.turn()


STRIP = 16


def apply_operator(field_ref, before_ref, after_ref, weight_ref, image_ref):
    width = field_ref.shape[1]

    def strip(k, carry):
        rows = pl.ds(pl.multiple_of(k * STRIP, STRIP), STRIP)
        sources = []
        for ref in (before_ref, field_ref, after_ref):
            value = ref[rows, :]
            sources.append(value)
            sources.append(jnp.concatenate([value[:, width // 2:], value[:, :width // 2]], axis=1))
        total = None
        for d, shift in enumerate((1, 0, width - 1)):
            part = weight_ref[6 * d:6 * d + 1, :] * sources[0]
            for m in range(1, 6):
                part = part + weight_ref[6 * d + m:6 * d + m + 1, :] * sources[m]
            if shift:
                part = pltpu.roll(part, shift, axis=1)
            total = part if total is None else total + part
        image_ref[rows, :] = total
        return carry

    lax.fori_loop(0, field_ref.shape[0] // STRIP, strip, 0)


def send_rows(copies, field_ref, before_ref, after_ref):
    return [copies.launch(field_ref, before_ref, beside(1)), copies.launch(field_ref, after_ref, beside(-1))]


RITZ_LAYOUT = (128, [("core", "scatter"), ("z", "scatter"), ("x", "exchange"), ("y", "exchange")])
GRAM_LAYOUTS = [
    (768, [("core", "scatter"), ("x", "scatter"), ("y", "scatter"), ("z", "exchange")]),
    (768, [("core", "scatter"), ("y", "scatter"), ("x", "scatter"), ("z", "exchange")]),
]
AXES = ("core", "x", "y", "z")


def start_kernel(modes_ref, dirs_ref, weight_ref, image_ref, dir_image_ref, ritz_ref, *scratch):
    before, after, dir_before, dir_after, local = scratch[:5]
    copies = Copies(*scratch[-2:])
    greet(AXES)
    halo = send_rows(copies, modes_ref, before, after)
    dir_halo = send_rows(copies, dirs_ref, dir_before, dir_after)
    for copy in halo:
        copy.wait_recv()
    apply_operator(modes_ref, before, after, weight_ref, image_ref)
    local[...] = product(modes_ref[...], image_ref[...], (1, 1))
    share = Share(RITZ_LAYOUT, 0, local, ritz_ref, scratch[5:-2], copies)
    share.begin()
    share.turn()
    for copy in dir_halo:
        copy.wait_recv()
    apply_operator(dirs_ref, dir_before, dir_after, weight_ref, dir_image_ref)
    through([share])
    copies.drain()


def search_kernel(modes_ref, images_ref, dirs_ref, dir_images_ref, ritz_ref, damping_ref, weight_ref,
                  search_ref, search_image_ref, sum_ref, *scratch):
    n = 128
    before, after, local = scratch[:3]
    rest = scratch[3:-2]
    half = len(rest) // 2
    copies = Copies(*scratch[-2:])
    greet(AXES)
    search = (images_ref[...] - product(ritz_ref[...], modes_ref[...])) * damping_ref[...]
    search_ref[...] = search
    halo = send_rows(copies, search_ref, before, after)

    def put(k, left_ref, right_ref):
        local[n * k:n * (k + 1)] = product(left_ref[...], right_ref[...], (1, 1))

    put(6, modes_ref, modes_ref)
    put(7, search_ref, modes_ref)
    put(8, search_ref, search_ref)
    put(9, dirs_ref, modes_ref)
    put(10, dirs_ref, search_ref)
    put(11, dirs_ref, dirs_ref)
    fields = Share(GRAM_LAYOUTS[0], 768, local, sum_ref, rest[:half], copies)
    fields.begin()
    put(0, modes_ref, images_ref)
    put(1, search_ref, images_ref)
    put(3, dirs_ref, images_ref)
    put(4, dir_images_ref, search_ref)
    put(5, dirs_ref, dir_images_ref)
    fields.turn()
    for copy in halo:
        copy.wait_recv()
    apply_operator(search_ref, before, after, weight_ref, search_image_ref)
    put(2, search_ref, search_image_ref)
    images = Share(GRAM_LAYOUTS[1], 0, local, sum_ref, rest[half:], copies)
    images.begin()
    through([fields, images])
    copies.drain()


def call_remote(kernel, name, collective_id, outs, landing, local_rows, layouts, operands, halos):
    scratch = [pltpu.VMEM((128, 512), jnp.float32)] * landing + [pltpu.VMEM((local_rows, 128), jnp.float32)]
    count = halos
    for layout in layouts:
        share_scratch, _, copies = plan(layout)
        scratch += share_scratch
        count += copies
    scratch += [pltpu.SemaphoreType.DMA((count,))] * 2
    vmem = pl.BlockSpec(memory_space=pltpu.VMEM)
    return pl.pallas_call(
        kernel,
        out_shape=tuple(jax.ShapeDtypeStruct(shape, jnp.float32) for shape in outs),
        in_specs=[vmem] * len(operands),
        out_specs=[vmem] * len(outs),
        scratch_shapes=scratch,
        compiler_params=pltpu.CompilerParams(
            collective_id=collective_id, has_side_effects=True, vmem_limit_bytes=32 << 20
        ),
        name=name,
    )(*operands)


offsets = [
    (a, b, c) for a in (-1, 0, 1) for b in (-1, 0, 1) for c in (-1, 0, 1) if (a, b, c) > (0, 0, 0)
]


def from_behind(block, axis, distance):
    devices = range(lax.axis_size(axis))
    route = [(i - distance, i) for i in devices if i - distance in devices]
    return lax.ppermute(block, axis, route)


def matmul(left, right):
    return jnp.dot(left, right, precision=lax.Precision.HIGHEST, preferred_element_type=jnp.float32)


def symmetric(matrix):
    return 0.5 * (matrix + matrix.T)


def product(left, right, over=(1, 0)):
    return lax.dot_general(
        left, right, (((over[0],), (over[1],)), ((), ())),
        precision=lax.Precision.HIGHEST, preferred_element_type=jnp.float32,
    )


SETTLED = 2e-3
MOST_STEPS = 10


def inverse_factor(matrix, step_ref, work_ref):
    n = matrix.shape[0]
    row = lax.broadcasted_iota(jnp.int32, (n, n), 0)
    col = lax.broadcasted_iota(jnp.int32, (n, n), 1)
    same = row == col
    unit = jnp.where(same, 1.0, 0.0)
    diag = jnp.where(same, matrix, 0.0)
    scale_row = lax.rsqrt(jnp.sum(diag, axis=0, keepdims=True))
    scale_col = lax.rsqrt(jnp.sum(diag, axis=1, keepdims=True))
    scaled = scale_col * matrix * scale_row

    def half(error):
        return jnp.where(row > col, error, jnp.where(same, 0.5 * error, 0.0))

    start = scaled - unit
    step_ref[...] = unit - half(start)

    def going(carry):
        count, size = carry
        return jnp.logical_and(count < MOST_STEPS, jnp.logical_not(size < SETTLED * SETTLED))

    def step(carry):
        count, _ = carry
        now = step_ref[...]
        error = product(product(now, scaled), now, (1, 1)) - unit
        step_ref[...] = now - product(half(error), now)
        return count + 1, jnp.sum(error * error)

    _, size = lax.while_loop(going, step, (jnp.int32(0), jnp.sum(start * start)))

    @pl.when(jnp.logical_not(size < SETTLED * SETTLED))
    def _():
        work_ref[...] = scaled
        step_ref[...] = unit

        def eliminate(j, carry):
            work, done = work_ref[...], step_ref[...]
            pivot_row = jnp.sum(jnp.where(row == j, work, 0.0), axis=0, keepdims=True)
            pivot_col = jnp.sum(jnp.where(col == j, work, 0.0), axis=1, keepdims=True)
            done_row = jnp.sum(jnp.where(row == j, done, 0.0), axis=0, keepdims=True)
            pivot = jnp.sum(jnp.where(same & (row == j), work, 0.0))
            factor = jnp.where(row > j, pivot_col / pivot, 0.0)
            work_ref[...] = work - factor * pivot_row
            done = done - factor * done_row
            step_ref[...] = jnp.where(row == j, done * lax.rsqrt(jnp.full((1, n), pivot)), done)
            return carry

        lax.fori_loop(0, n, eliminate, 0)

    return step_ref[...] * scale_row


def pencil_kernel(sum_ref, coeff_ref, ritz_ref, image_ref, inverse_ref, step_ref, work_ref):
    n = 128

    def block(k):
        return sum_ref[n * k:n * (k + 1)]

    row = lax.broadcasted_iota(jnp.int32, (n, n), 0)
    col = lax.broadcasted_iota(jnp.int32, (n, n), 1)
    same = row == col
    place = [(0, 0), (1, 0), (1, 1), (2, 0), (2, 1), (2, 2)]
    across, down = [], []
    for k in (6, 8, 11):
        diag = jnp.where(same, block(k), 0.0)
        across.append(lax.rsqrt(jnp.sum(diag, axis=0, keepdims=True) + 1e-06))
        down.append(lax.rsqrt(jnp.sum(diag, axis=1, keepdims=True) + 1e-06))
    normed = {}
    for k, (i, j) in enumerate(place):
        image = block(k)
        field = block(6 + k)
        if i == j:
            image = 0.5 * (image + image.T)
            field = 0.5 * (field + field.T)
        image_ref[n * i:n * (i + 1), n * j:n * (j + 1)] = image
        if i != j:
            image_ref[n * j:n * (j + 1), n * i:n * (i + 1)] = image.T
        normed[i, j] = down[i] * field * across[j]

    inverse_0 = inverse_factor(normed[0, 0], step_ref, work_ref)
    lower_10 = product(normed[1, 0], inverse_0, (1, 1))
    lower_20 = product(normed[2, 0], inverse_0, (1, 1))
    inverse_1 = inverse_factor(normed[1, 1] - product(lower_10, lower_10, (1, 1)), step_ref, work_ref)
    lower_21 = product(normed[2, 1] - product(lower_20, lower_10, (1, 1)), inverse_1, (1, 1))
    rest = normed[2, 2] - product(lower_20, lower_20, (1, 1)) - product(lower_21, lower_21, (1, 1))
    inverse_10 = -product(inverse_1, product(lower_10, inverse_0))
    inner_20 = product(lower_20, inverse_0) + product(lower_21, inverse_10)
    inner_21 = product(lower_21, inverse_1)
    inverse_2 = inverse_factor(rest, step_ref, work_ref)
    inverse_ref[...] = jnp.zeros((3 * n, 3 * n), jnp.float32)
    inverse_ref[0:n, 0:n] = inverse_0 * across[0]
    inverse_ref[n:2 * n, 0:n] = inverse_10 * across[0]
    inverse_ref[n:2 * n, n:2 * n] = inverse_1 * across[1]
    inverse_ref[2 * n:, 0:n] = -product(inverse_2, inner_20) * across[0]
    inverse_ref[2 * n:, n:2 * n] = -product(inverse_2, inner_21) * across[1]
    inverse_ref[2 * n:, 2 * n:] = inverse_2 * across[2]
    reduced = product(product(inverse_ref[...], image_ref[...]), inverse_ref[...], (1, 1))
    shift = 2.0 * jnp.max(jnp.sum(jnp.abs(reduced), axis=1, keepdims=True))
    reduced = reduced * (1.0 / jnp.full((1, 3 * n), shift))
    tall_row = lax.broadcasted_iota(jnp.int32, (3 * n, n), 0)
    tall_col = lax.broadcasted_iota(jnp.int32, (3 * n, n), 1)
    iterate = jnp.where(tall_row == tall_col, 1.0, 0.0) - reduced[:, :n]
    for _ in range(QSTEPS - 1):
        iterate = iterate - product(reduced, iterate)
    factor = inverse_factor(product(iterate, iterate, (0, 0)), step_ref, work_ref)
    iterate = product(iterate, factor, (1, 1))
    coeffs = product(inverse_ref[...], iterate, (0, 0))
    coeff_ref[...] = coeffs
    quotient = product(coeffs, product(image_ref[...], coeffs), (0, 0))
    ritz_ref[...] = 0.5 * (quotient + quotient.T)


def solve_pencil(summed):
    n = 128
    square = pltpu.VMEM((3 * n, 3 * n), jnp.float32)
    small = pltpu.VMEM((n, n), jnp.float32)
    return pl.pallas_call(
        pencil_kernel,
        out_shape=(jax.ShapeDtypeStruct((3 * n, n), jnp.float32), jax.ShapeDtypeStruct((n, n), jnp.float32)),
        in_specs=[pl.BlockSpec(memory_space=pltpu.VMEM)],
        out_specs=[pl.BlockSpec(memory_space=pltpu.VMEM)] * 2,
        scratch_shapes=[square, square, small, small],
        compiler_params=pltpu.CompilerParams(vmem_limit_bytes=32 << 20),
        name="pencil",
    )(summed)


def row_weights(own, before, first, last, rate):
    def inner(block, dz, dx):
        padded = jnp.pad(block, ((1, 1), (1, 1)))
        return padded[1 - dz:1 - dz + NZ, 1 - dx:1 - dx + NX]

    z = lax.broadcasted_iota(jnp.int32, (NZ, NX), 0)
    x = lax.broadcasted_iota(jnp.int32, (NZ, NX), 1)
    table = {}
    for which, (dy, dz, dx) in enumerate(offsets):
        inside = (z + dz >= 0) & (z + dz < NZ) & (x + dx >= 0) & (x + dx < NX)
        if dy:
            inside = inside & jnp.logical_not(last)
        table[dy, dz, dx] = jnp.where(inside, own[which], 0.0)
        if dy:
            table[-dy, -dz, -dx] = jnp.where(first, 0.0, inner(before[which], dz, dx))
        else:
            table[-dy, -dz, -dx] = inner(own[which], dz, dx)
    degree = sum(table.values())
    rows = []
    for dx in (-1, 0, 1):
        for dy in (-1, 0, 1):
            if (dy, dx) == (0, 0):
                same = degree + rate
            else:
                same = -table[dy, 0, dx]
            other = -(table[dy, 1, dx] + table[dy, -1, dx])
            rows += [jnp.roll(block.reshape(NZ * NX), dx) for block in (same, other)]
    return jnp.stack(rows)


def on_device(start_modes, start_dirs, coupling, relax_class, relaxivity):
    local_voxels = coupling.shape[1]
    match = relax_class[:, None] == jnp.arange(relaxivity.shape[0], dtype=jnp.int32)[None, :]
    voxel_rate = jnp.sum(jnp.where(match, relaxivity[None, :], jnp.float32(0.0)), axis=1)
    damping = 1.0 / (1.0 + voxel_rate)
    own = coupling.reshape(HALF, NZ, NX)
    before = from_behind(own, ("vox", "col"), 1)
    position = lax.axis_index(("vox", "col"))
    device_count = lax.axis_size(("vox", "col"))
    weights = row_weights(own, before, position == 0, position == device_count - 1, voxel_rate.reshape(NZ, NX))

    modes, dirs = (
        lax.all_to_all(start_modes, "col", split_axis=1, concat_axis=0, tiled=True),
        lax.all_to_all(start_dirs, "col", split_axis=1, concat_axis=0, tiled=True),
    )
    count = modes.shape[0]
    row, small = (count, local_voxels), (count, count)
    images, dir_images, ritz = call_remote(
        start_kernel, "start", 1, (row, row, small), 4, 128, [RITZ_LAYOUT], (modes, dirs, weights), 4
    )
    ritz = symmetric(ritz)
    for iteration in range(ITERS):
        search, search_images, summed = call_remote(
            search_kernel, "search", 2, (row, row, (12 * count, count)), 2, 12 * count, GRAM_LAYOUTS,
            (modes, images, dirs, dir_images, ritz, damping[None, :], weights), 2,
        )
        basis = jnp.concatenate([modes, search, dirs], axis=0)
        basis_images = jnp.concatenate([images, search_images, dir_images], axis=0)
        coeffs, ritz = solve_pencil(summed)
        modes = matmul(coeffs.T, basis)
        images = matmul(coeffs.T, basis_images)
        dirs = matmul(coeffs[count:].T, basis[count:])
        dir_images = matmul(coeffs[count:].T, basis_images[count:])
    total_voxels = device_count * local_voxels
    scaled = modes * math.sqrt(total_voxels)
    modes_out = lax.all_to_all(scaled, "col", split_axis=0, concat_axis=1, tiled=True)
    return (modes_out, ritz)


def solution(mesh):
    in_specs = (P("col", "vox"), P("col", "vox"), P(None, ("vox", "col")), P(("vox", "col")), P())
    out_specs = (P("col", "vox"), P())
    return jax.shard_map(
        on_device, mesh=mesh, in_specs=in_specs, out_specs=out_specs, check_vma=False
    )
```

time: 322 us -> 281 us (0.87); the launches traced: 316 us -> 281 us
  starting transfers between devices: 35.7 us -> 13.6 us
  other arithmetic: 29.2 us -> 9.21 us
  Pallas kernels: 216 us -> 230 us
  matrix products: 11.1 us -> 2.91 us
  local copies, waits for them, and re-layouts: 7.46 us -> 12.2 us
    ppermute x8 -> x0, starting transfers between devices: 22.7 us -> none  [the longest x4 14 us: extended_2(): lax.ppermute(lax.slice_in_dim(block, block.shape[dim] - width, None, axis...]
    pallas_call x3, Pallas kernels: 98.7 us -> 112 us  [call_remote(): pl.pallas_call(kernel, out_shape=tuple((jax.ShapeDtypeStruct(shape, jnp.f...]
    add x4 -> x0, other arithmetic: 13.3 us -> none  [the longest x3 13.2 us: neighbour_sum(): total = total + back[None] * behind]
    dot_general x19 -> x5, matrix products: 11.1 us -> 2.91 us  [matmul(): jnp.dot(left, right, precision=lax.Precision.HIGHEST, preferred_element_t...]
    slice x13 -> x18, local copies, waits for them, and re-layouts: 1.11 us -> 7.22 us  [row_weights(): rows += [jnp.roll(block.reshape(NZ * NX), dx) for block in (same, other)]]
    sub x4 -> x0, other arithmetic: 4.65 us -> none  [operate(): diagonal[None, :] * field]
    concatenate x6 -> x12, other arithmetic: 9.36 us -> 8.41 us  [row_weights(): rows += [jnp.roll(block.reshape(NZ * NX), dx) for block in (same, other)]]
  transfers between devices with their start and end apart: 11 -> 3, of which waited for: 3 -> 1; matrix products, arithmetic and copies ran while one was open for 8% -> 7% of each run, Pallas kernels for 9% -> 0%
where the time goes in v3:
time: 281 us
  Pallas kernels  230 us (82%)
  starting transfers between devices  13.6 us (5%)
  local copies, waits for them, and re-layouts  12.2 us (4%)
  other arithmetic  9.21 us (3%)
  blocking collectives  8.97 us (3%)
  waiting for transfers between devices  3.06 us (1%)
  matrix products  2.91 us (1%)
    pallas_call x2, Pallas kernels, solve_pencil(): pl.pallas_call(pencil_kernel, out_shape=(jax.ShapeDtypeStruct((3 * n, n),...  118 us
    pallas_call x3, Pallas kernels, call_remote(): pl.pallas_call(kernel, out_shape=tuple((jax.ShapeDtypeStruct(shape, jnp.f...  112 us
    all_to_all x1, blocking collectives, on_device(): lax.all_to_all(scaled, 'col', split_axis=0, concat_axis=1, tiled=True)  8.97 us
    concatenate x12, other arithmetic, row_weights(): rows += [jnp.roll(block.reshape(NZ * NX), dx) for block in (same, other)]  8.41 us
    slice x18, local copies, waits for them, and re-layouts, row_weights(): rows += [jnp.roll(block.reshape(NZ * NX), dx) for block in (same, other)]  7.22 us
  transfers between devices with their start and end apart: 3, of which 1 were waited for; matrix products, arithmetic and copies ran while one was open for 7% of the time, Pallas kernels for 0%

profile of v3, /device:TPU:1, one launch (start us, length us, event | category | flops | bytes accessed | tf_op | source)
XLA Modules:
  0.0 280.5 jit_solution(17206754626194651107)
XLA Ops:
  0.6 0.8 reshape.282
  1.4 4.5 %collective-permute-start = (f32[13,2,256]{2,1,0:T(2,128)S(1)}, f32[13,2,256]{2,1,0:T(2,128)S(1)}, u32[]{:S(2)}, u32[]{:S(2)}) collective-permute-start(f32[13,2,256]{2,1,0:T(2,128)S(1)} %reshape.282), channel_id=1, source_target_pairs={{0,1},{1,2},{2,3},{3,4},{4,5},{5,6},{6,7},{7,8},{8,9},{9,10},{10,1... | collective-permute-start | bytes 79880 | tf_op jit(solution)/shard_map/ppermute | solution.py:285
  5.9 1.7 copy.35
  7.6 4.3 %all-to-all-start = ((f32[16,8,512]{2,0,1:T(8,128)}), f32[16,8,512]{2,0,1:T(8,128)S(1)}, u32[]{:S(2)}, u32[]{:S(2)}) async-start(f32[16,8,512]{2,0,1:T(8,128)} %bitcast.114), calls=%async_computation | async-start | bytes 524288 | tf_op jit(solution)/shard_map/all_to_all | solution.py:476
  12.0 0.1 fusion.28
  12.1 0.5 slice.229
  12.8 0.5 slice.225
  13.4 0.1 fusion.67
  13.6 0.5 slice.217
  14.3 0.6 slice.222
  15.0 0.6 copy-done.2
  15.7 0.7 slice.254
  16.4 0.6 slice.258
  17.0 0.6 slice.260
  17.5 0.6 slice.256
  18.2 0.7 pad_maximum_fusion.5
  18.9 0.6 pad_maximum_fusion.4
  19.5 0.6 pad_maximum_fusion.10
  20.1 0.7 pad_maximum_fusion.8
  20.8 0.7 pad_maximum_fusion.11
  21.5 0.7 pad_maximum_fusion.2
  22.3 0.7 pad_maximum_fusion.9
  22.9 0.8 pad_maximum_fusion.3
  23.8 0.7 copy.34
  24.6 0.5 slice.213
  25.3 0.7 pad_maximum_fusion.1
  26.0 0.6 slice.252
  26.6 0.1 add_bitcast_fusion
  26.7 4.8 %all-to-all-start.1 = ((f32[16,8,512]{2,0,1:T(8,128)}), f32[16,8,512]{2,0,1:T(8,128)S(1)}, u32[]{:S(2)}, u32[]{:S(2)}) async-start(f32[16,8,512]{2,0,1:T(8,128)} %bitcast.113), calls=%async_computation.1 | async-start | bytes 524288 | tf_op jit(solution)/shard_map/all_to_all | solution.py:477
  31.6 0.7 pad_maximum_fusion.7
  32.3 0.5 slice.207
  32.9 0.6 slice.250
  33.5 0.7 pad_maximum_fusion.6
  34.2 0.7 pad_maximum_fusion
  34.9 0.1 stack.66.weight_ref
  35.0 3.1 %all-to-all-done.1 = f32[16,8,512]{2,0,1:T(8,128)S(1)} async-done(((f32[16,8,512]{2,0,1:T(8,128)}), f32[16,8,512]{2,0,1:T(8,128)S(1)}, u32[]{:S(2)}, u32[]{:S(2)}) %all-to-all-start.1) | async-done | bytes 262176 | tf_op jit(solution)/shard_map/all_to_all | solution.py:477
  38.1 35.2 %start.1 = (f32[128,512]{1,0:T(8,128)S(1)}, f32[128,512]{1,0:T(8,128)S(1)}, f32[128,128]{1,0:T(8,128)S(1)}) custom-call(f32[128,512]{1,0:T(8,128)S(1)} %bitcast.125, f32[128,512]{1,0:T(8,128)S(1)} %bitcast.121, f32[18,512]{1,0:T(8,128)S(1)} %stack.66.weight_ref), custom_call_target="tpu_custom_call" | custom-call | tf_op jit(solution)/shard_map/start/pallas_call | solution.py:264
  73.4 37.3 %search.2 = (f32[128,512]{1,0:T(8,128)S(1)}, f32[128,512]{1,0:T(8,128)S(1)}, f32[1536,128]{1,0:T(8,128)S(1)}) custom-call(f32[128,512]{1,0:T(8,128)S(1)} %bitcast.126, f32[128,512]{1,0:T(8,128)S(1)} %get-tuple-element.14.images_ref, f32[128,512]{1,0:T(8,128)S(1)} %bitcast.122, f32[128,512]{1,0:T(8,128)S(1)} %get-tuple-element.15.dir_images_ref, ...), custom_call_target="tpu_custom_call" | custom-call | tf_op jit(solution)/shard_map/search/pallas_call | solution.py:264
  110.8 98.4 %pencil.2 = (f32[384,128]{1,0:T(8,128)S(1)}, f32[128,128]{1,0:T(8,128)S(1)}) custom-call(f32[1536,128]{1,0:T(8,128)S(1)} %get-tuple-element.17.sum_ref), custom_call_target="tpu_custom_call" | custom-call | tf_op jit(solution)/shard_map/pencil/pallas_call | solution.py:423
  209.2 0.7 fusion.modes_ref
  209.9 0.5 fusion.17.dirs_ref
  210.3 0.7 fusion.6.images_ref
  211.0 0.5 fusion.21.dir_images_ref
  211.5 39.5 %search.3 = (f32[128,512]{1,0:T(8,128)S(1)}, f32[128,512]{1,0:T(8,128)}, f32[1536,128]{1,0:T(8,128)S(1)}) custom-call(f32[128,512]{1,0:T(8,128)S(1)} %fusion.modes_ref, f32[128,512]{1,0:T(8,128)S(1)} %fusion.6.images_ref, f32[128,512]{1,0:T(8,128)S(1)} %fusion.17.dirs_ref, f32[128,512]{1,0:T(8,128)S(1)} %fusion.21.dir_images_ref, ...), custom_call_target="tpu_custom_call" | custom-call | tf_op jit(solution)/shard_map/search/pallas_call | solution.py:264
  251.0 19.2 %pencil.3 = (f32[384,128]{1,0:T(8,128)S(1)}, f32[128,128]{1,0:T(8,128)}) custom-call(f32[1536,128]{1,0:T(8,128)S(1)} %get-tuple-element.22.sum_ref), custom_call_target="tpu_custom_call" | custom-call | tf_op jit(solution)/shard_map/pencil/pallas_call | solution.py:423
  270.2 0.7 convolution_multiply_fusion
  270.9 9.0 %all_to_all.57 = f32[8,16,512]{2,1,0:T(8,128)S(1)} all-to-all(f32[8,16,512]{2,1,0:T(8,128)S(1)} %bitcast.130), channel_id=1, replica_groups=mesh['vox'=32,'col'=8] {'col'}, dimensions={0} | all-to-all | bytes 524288 | tf_op jit(solution)/shard_map/all_to_all | solution.py:499
  279.8 0.7 copy.17
  (69 shorter events, 1.4 us)
Async XLA Ops:
  1.4 23.1 %collective-permute-start = (f32[13,2,256]{2,1,0:T(2,128)S(1)}, f32[13,2,256]{2,1,0:T(2,128)S(1)}, u32[]{:S(2)}, u32[]{:S(2)}) collective-permute-start(f32[13,2,256]{2,1,0:T(2,128)S(1)} %reshape.282), channel_id=1, source_target_pairs={{0,1},{1,2},{2,3},{3,4},{4,5},{5,6},{6,7},{7,8},{8,9},{9,10},{10,1... | collective-permute-start | bytes 79880 | tf_op jit(solution)/shard_map/ppermute | solution.py:285
  7.6 4.5 %copy-start.1 = (f32[13,512]{1,0:T(8,128)S(1)}, f32[13,512]{1,0:T(8,128)}, u32[]{:S(2)}) copy-start(f32[13,512]{1,0:T(8,128)} %param.7) | copy-start | bytes 79876
  7.6 19.1 %all-to-all-start = ((f32[16,8,512]{2,0,1:T(8,128)}), f32[16,8,512]{2,0,1:T(8,128)S(1)}, u32[]{:S(2)}, u32[]{:S(2)}) async-start(f32[16,8,512]{2,0,1:T(8,128)} %bitcast.114), calls=%async_computation | async-start | bytes 524288 | tf_op jit(solution)/shard_map/all_to_all | solution.py:476
  11.9 12.0 %copy-start = (f32[16,4096]{1,0:T(8,128)S(1)}, f32[16,4096]{1,0:T(8,128)}, u32[]{:S(2)}) copy-start(f32[16,4096]{1,0:T(8,128)} %param.6) | copy-start | bytes 786436
  14.9 0.7 copy-start.2
  14.9 0.7 copy-start.3
  26.7 11.3 %all-to-all-start.1 = ((f32[16,8,512]{2,0,1:T(8,128)}), f32[16,8,512]{2,0,1:T(8,128)S(1)}, u32[]{:S(2)}, u32[]{:S(2)}) async-start(f32[16,8,512]{2,0,1:T(8,128)} %bitcast.113), calls=%async_computation.1 | async-start | bytes 524288 | tf_op jit(solution)/shard_map/all_to_all | solution.py:477

commit v4 on v3

--- a/solution.py
+++ b/solution.py
@@ -43,14 +43,22 @@
     return {"vox": lax.div(place, 8), "col": lax.rem(place, 8)}
 
 
-def greet(axes):
+def column(step):
+    return {"col": lax.rem(lax.axis_index("col") + step, 8)}
+
+
+def along(axes):
+    return [peer(axis, step) for axis in axes for step in range(1, SIZES[axis])]
+
+
+def hail(devices):
     barrier = pltpu.get_barrier_semaphore()
-    devices = [beside(1), beside(-1)]
-    for axis in axes:
-        devices += [peer(axis, step) for step in range(1, SIZES[axis])]
     for device in devices:
         pl.semaphore_signal(barrier, inc=1, device_id=device, device_id_type=pl.DeviceIdType.MESH)
-    pl.semaphore_wait(barrier, len(devices))
+
+
+def heard(devices):
+    pl.semaphore_wait(pltpu.get_barrier_semaphore(), len(devices))
 
 
 class Copies:
@@ -188,25 +196,93 @@
 RITZ_LAYOUT = (128, [("core", "scatter"), ("z", "scatter"), ("x", "exchange"), ("y", "exchange")])
 GRAM_LAYOUTS = [
     (768, [("core", "scatter"), ("x", "scatter"), ("y", "scatter"), ("z", "exchange")]),
-    (768, [("core", "scatter"), ("y", "scatter"), ("x", "scatter"), ("z", "exchange")]),
+    (512, [("core", "scatter"), ("y", "scatter"), ("x", "scatter"), ("z", "exchange")]),
+    RITZ_LAYOUT,
 ]
+GRAM_ROWS = 1408
 AXES = ("core", "x", "y", "z")
-
-
-def start_kernel(modes_ref, dirs_ref, weight_ref, image_ref, dir_image_ref, ritz_ref, *scratch):
-    before, after, dir_before, dir_after, local = scratch[:5]
+COLUMNS = range(1, 8)
+
+
+def fill_weights(own_ref, before_ref, rate, weight_ref):
+    width = own_ref.shape[1]
+    lane = lax.broadcasted_iota(jnp.int32, (1, width), 1)
+    z, x = lane // NX, lane % NX
+    place = lax.axis_index("vox") * 8 + lax.axis_index("col")
+    first, last = place == 0, place == 255
+
+    def shifted(value, distance):
+        distance = distance % width
+        return pltpu.roll(value, distance, axis=1) if distance else value
+
+    def within(dz, dx):
+        return (z + dz >= 0) & (z + dz < NZ) & (x + dx >= 0) & (x + dx < NX)
+
+    table = {}
+    for which, (dy, dz, dx) in enumerate(offsets):
+        ahead = jnp.where(within(dz, dx), own_ref[which:which + 1, :], 0.0)
+        source = before_ref if dy else own_ref
+        back = jnp.where(within(-dz, -dx), shifted(source[which:which + 1, :], dz * NX + dx), 0.0)
+        if dy:
+            ahead = ahead * jnp.where(last, 0.0, 1.0)
+            back = back * jnp.where(first, 0.0, 1.0)
+        table[dy, dz, dx] = ahead
+        table[-dy, -dz, -dx] = back
+    degree = sum(table.values())
+    k = 0
+    for dx in (-1, 0, 1):
+        for dy in (-1, 0, 1):
+            same = degree + rate if (dy, dx) == (0, 0) else -table[dy, 0, dx]
+            other = -(table[dy, 1, dx] + table[dy, -1, dx])
+            for value in (same, other):
+                weight_ref[k:k + 1, :] = shifted(value, dx)
+                k += 1
+
+
+def send_columns(copies, group_ref, row_ref):
+    me = lax.axis_index("col")
+    count, width = group_ref.shape[0], row_ref.shape[1]
+    mine = pl.ds(pl.multiple_of(me * count, 8), count)
+    sent = []
+    for step in COLUMNS:
+        voxels = pl.ds(pl.multiple_of(lax.rem(me + step, 8) * width, 128), width)
+        sent.append(copies.launch(group_ref.at[:, voxels], row_ref.at[mine], column(step)))
+    row_ref[mine, :] = group_ref[:, pl.ds(pl.multiple_of(me * width, 128), width)]
+    return sent
+
+
+def start_kernel(group_ref, dir_group_ref, coupling_ref, class_ref, relaxivity_ref,
+                 modes_ref, dirs_ref, image_ref, dir_image_ref, weight_ref, damping_ref, ritz_ref, *scratch):
+    before, after, dir_before, dir_after, coupling_before, local = scratch[:6]
     copies = Copies(*scratch[-2:])
-    greet(AXES)
+    near = [beside(1), beside(-1)] + [column(step) for step in COLUMNS] + along(("y", "z"))
+    near += along(("core", "x"))
+    hail(near)
+    rate = jnp.zeros(class_ref.shape, jnp.float32)
+    for k in range(relaxivity_ref.shape[1]):
+        rate = rate + jnp.where(class_ref[...] == k, relaxivity_ref[:, k:k + 1], 0.0)
+    damping_ref[...] = 1.0 / (1.0 + rate)
+    heard(near)
+    coupled = copies.launch(coupling_ref, coupling_before, beside(1))
+    arriving = send_columns(copies, group_ref, modes_ref)
+    coupled.wait_recv()
+    fill_weights(coupling_ref, coupling_before, rate, weight_ref)
+    for copy in arriving:
+        copy.wait_recv()
     halo = send_rows(copies, modes_ref, before, after)
-    dir_halo = send_rows(copies, dirs_ref, dir_before, dir_after)
+    arriving = send_columns(copies, dir_group_ref, dirs_ref)
     for copy in halo:
         copy.wait_recv()
     apply_operator(modes_ref, before, after, weight_ref, image_ref)
     local[...] = product(modes_ref[...], image_ref[...], (1, 1))
-    share = Share(RITZ_LAYOUT, 0, local, ritz_ref, scratch[5:-2], copies)
+    share = Share(RITZ_LAYOUT, 0, local, ritz_ref, scratch[6:-2], copies)
     share.begin()
+    for copy in arriving:
+        copy.wait_recv()
+    halo = send_rows(copies, dirs_ref, dir_before, dir_after)
     share.turn()
-    for copy in dir_halo:
+    share.turn()
+    for copy in halo:
         copy.wait_recv()
     apply_operator(dirs_ref, dir_before, dir_after, weight_ref, dir_image_ref)
     through([share])
@@ -217,44 +293,78 @@
                   search_ref, search_image_ref, sum_ref, *scratch):
     n = 128
     before, after, local = scratch[:3]
-    rest = scratch[3:-2]
-    half = len(rest) // 2
+    rest = list(scratch[3:-2])
     copies = Copies(*scratch[-2:])
-    greet(AXES)
-    search = (images_ref[...] - product(ritz_ref[...], modes_ref[...])) * damping_ref[...]
-    search_ref[...] = search
+    near = [beside(1), beside(-1)] + along(AXES)
+    hail(near)
+    search_ref[...] = (images_ref[...] - product(ritz_ref[...], modes_ref[...])) * damping_ref[...]
+    heard(near)
     halo = send_rows(copies, search_ref, before, after)
-
-    def put(k, left_ref, right_ref):
-        local[n * k:n * (k + 1)] = product(left_ref[...], right_ref[...], (1, 1))
-
-    put(6, modes_ref, modes_ref)
-    put(7, search_ref, modes_ref)
-    put(8, search_ref, search_ref)
-    put(9, dirs_ref, modes_ref)
-    put(10, dirs_ref, search_ref)
-    put(11, dirs_ref, dirs_ref)
-    fields = Share(GRAM_LAYOUTS[0], 768, local, sum_ref, rest[:half], copies)
-    fields.begin()
-    put(0, modes_ref, images_ref)
-    put(1, search_ref, images_ref)
-    put(3, dirs_ref, images_ref)
-    put(4, dir_images_ref, search_ref)
-    put(5, dirs_ref, dir_images_ref)
-    fields.turn()
+    shares, start = [], 0
+    for layout in GRAM_LAYOUTS:
+        used = 2 * len(layout[1])
+        shares.append(Share(layout, start, local, sum_ref, rest[:used], copies))
+        rest, start = rest[used:], start + layout[0]
+
+    def between(left_ref, right_ref):
+        return product(left_ref[...], right_ref[...], (1, 1))
+
+    def put(k, value):
+        local[n * k:n * (k + 1)] = value
+
+    row = lax.broadcasted_iota(jnp.int32, (n, n), 0)
+    col = lax.broadcasted_iota(jnp.int32, (n, n), 1)
+    put(0, between(search_ref, modes_ref))
+    put(1, between(dirs_ref, modes_ref))
+    put(2, between(dirs_ref, search_ref))
+    put(3, between(search_ref, images_ref))
+    put(4, between(dirs_ref, images_ref))
+    put(5, between(dir_images_ref, search_ref))
+    shares[0].begin()
+    ends = jnp.zeros((n, n), jnp.float32)
+    for k, (field_ref, field_image_ref) in enumerate(((modes_ref, images_ref), (dirs_ref, dir_images_ref))):
+        field = between(field_ref, field_ref)
+        put(6 + k, jnp.where(row >= col, between(field_ref, field_image_ref), field))
+        ends = jnp.where(row == k, jnp.sum(jnp.where(row == col, field, 0.0), axis=0, keepdims=True), ends)
+    put(8, between(search_ref, search_ref))
+    put(9, ends)
+    shares[1].begin()
+    shares[0].turn()
     for copy in halo:
         copy.wait_recv()
     apply_operator(search_ref, before, after, weight_ref, search_image_ref)
-    put(2, search_ref, search_image_ref)
-    images = Share(GRAM_LAYOUTS[1], 0, local, sum_ref, rest[half:], copies)
-    images.begin()
-    through([fields, images])
+    put(10, between(search_ref, search_image_ref))
+    shares[2].begin()
+    shares[1].turn()
+    through(shares)
     copies.drain()
 
 
-def call_remote(kernel, name, collective_id, outs, landing, local_rows, layouts, operands, halos):
-    scratch = [pltpu.VMEM((128, 512), jnp.float32)] * landing + [pltpu.VMEM((local_rows, 128), jnp.float32)]
-    count = halos
+def finish_kernel(coeff_ref, modes_ref, search_ref, dirs_ref, group_ref, *scratch):
+    n = 128
+    copies = Copies(*scratch[-2:])
+    final = scratch[0]
+    near = [column(step) for step in COLUMNS]
+    hail(near)
+    total = product(coeff_ref[0:n], modes_ref[...], (0, 0)) + product(coeff_ref[n:2 * n], search_ref[...], (0, 0))
+    final[...] = (total + product(coeff_ref[2 * n:], dirs_ref[...], (0, 0))) * math.sqrt(256 * final.shape[1])
+    heard(near)
+    me = lax.axis_index("col")
+    count, width = group_ref.shape[0], final.shape[1]
+    voxels = pl.ds(pl.multiple_of(me * width, 128), width)
+    arriving = []
+    for step in COLUMNS:
+        other = pl.ds(pl.multiple_of(lax.rem(me + step, 8) * count, 8), count)
+        arriving.append(copies.launch(final.at[other], group_ref.at[:, voxels], column(step)))
+    group_ref[:, voxels] = final[pl.ds(pl.multiple_of(me * count, 8), count), :]
+    for copy in arriving:
+        copy.wait_recv()
+    copies.drain()
+
+
+def call_remote(kernel, name, collective_id, outs, scratch, layouts, operands, extra):
+    scratch = [pltpu.VMEM(shape, jnp.float32) for shape in scratch]
+    count = extra
     for layout in layouts:
         share_scratch, _, copies = plan(layout)
         scratch += share_scratch
@@ -265,7 +375,7 @@
         kernel,
         out_shape=tuple(jax.ShapeDtypeStruct(shape, jnp.float32) for shape in outs),
         in_specs=[vmem] * len(operands),
-        out_specs=[vmem] * len(outs),
+        out_specs=(vmem,) * len(outs),
         scratch_shapes=scratch,
         compiler_params=pltpu.CompilerParams(
             collective_id=collective_id, has_side_effects=True, vmem_limit_bytes=32 << 20
@@ -277,12 +387,6 @@
 offsets = [
     (a, b, c) for a in (-1, 0, 1) for b in (-1, 0, 1) for c in (-1, 0, 1) if (a, b, c) > (0, 0, 0)
 ]
-
-
-def from_behind(block, axis, distance):
-    devices = range(lax.axis_size(axis))
-    route = [(i - distance, i) for i in devices if i - distance in devices]
-    return lax.ppermute(block, axis, route)
 
 
 def matmul(left, right):
@@ -365,23 +469,28 @@
     row = lax.broadcasted_iota(jnp.int32, (n, n), 0)
     col = lax.broadcasted_iota(jnp.int32, (n, n), 1)
     same = row == col
-    place = [(0, 0), (1, 0), (1, 1), (2, 0), (2, 1), (2, 2)]
-    across, down = [], []
-    for k in (6, 8, 11):
-        diag = jnp.where(same, block(k), 0.0)
+    def mirrored(lower):
+        return jnp.where(row >= col, lower, lower.T)
+
+    ends = sum_ref[9 * n:9 * n + 8]
+    searched = block(10)
+    images = [mirrored(block(6)), 0.5 * (searched + searched.T), mirrored(block(7))]
+    fields = [mirrored(block(6).T), mirrored(block(8)), mirrored(block(7).T)]
+    fields[0] = jnp.where(same, ends[0:1], fields[0])
+    fields[2] = jnp.where(same, ends[1:2], fields[2])
+    across, down, normed = [], [], {}
+    for field in fields:
+        diag = jnp.where(same, field, 0.0)
         across.append(lax.rsqrt(jnp.sum(diag, axis=0, keepdims=True) + 1e-06))
         down.append(lax.rsqrt(jnp.sum(diag, axis=1, keepdims=True) + 1e-06))
-    normed = {}
-    for k, (i, j) in enumerate(place):
-        image = block(k)
-        field = block(6 + k)
-        if i == j:
-            image = 0.5 * (image + image.T)
-            field = 0.5 * (field + field.T)
+    for i in range(3):
+        image_ref[n * i:n * (i + 1), n * i:n * (i + 1)] = images[i]
+        normed[i, i] = down[i] * fields[i] * across[i]
+    for k, (i, j) in enumerate(((1, 0), (2, 0), (2, 1))):
+        image = block(3 + k)
         image_ref[n * i:n * (i + 1), n * j:n * (j + 1)] = image
-        if i != j:
-            image_ref[n * j:n * (j + 1), n * i:n * (i + 1)] = image.T
-        normed[i, j] = down[i] * field * across[j]
+        image_ref[n * j:n * (j + 1), n * i:n * (i + 1)] = image.T
+        normed[i, j] = down[i] * block(k) * across[j]
 
     inverse_0 = inverse_factor(normed[0, 0], step_ref, work_ref)
     lower_10 = product(normed[1, 0], inverse_0, (1, 1))
@@ -431,72 +540,32 @@
     )(summed)
 
 
-def row_weights(own, before, first, last, rate):
-    def inner(block, dz, dx):
-        padded = jnp.pad(block, ((1, 1), (1, 1)))
-        return padded[1 - dz:1 - dz + NZ, 1 - dx:1 - dx + NX]
-
-    z = lax.broadcasted_iota(jnp.int32, (NZ, NX), 0)
-    x = lax.broadcasted_iota(jnp.int32, (NZ, NX), 1)
-    table = {}
-    for which, (dy, dz, dx) in enumerate(offsets):
-        inside = (z + dz >= 0) & (z + dz < NZ) & (x + dx >= 0) & (x + dx < NX)
-        if dy:
-            inside = inside & jnp.logical_not(last)
-        table[dy, dz, dx] = jnp.where(inside, own[which], 0.0)
-        if dy:
-            table[-dy, -dz, -dx] = jnp.where(first, 0.0, inner(before[which], dz, dx))
-        else:
-            table[-dy, -dz, -dx] = inner(own[which], dz, dx)
-    degree = sum(table.values())
-    rows = []
-    for dx in (-1, 0, 1):
-        for dy in (-1, 0, 1):
-            if (dy, dx) == (0, 0):
-                same = degree + rate
-            else:
-                same = -table[dy, 0, dx]
-            other = -(table[dy, 1, dx] + table[dy, -1, dx])
-            rows += [jnp.roll(block.reshape(NZ * NX), dx) for block in (same, other)]
-    return jnp.stack(rows)
-
-
 def on_device(start_modes, start_dirs, coupling, relax_class, relaxivity):
     local_voxels = coupling.shape[1]
-    match = relax_class[:, None] == jnp.arange(relaxivity.shape[0], dtype=jnp.int32)[None, :]
-    voxel_rate = jnp.sum(jnp.where(match, relaxivity[None, :], jnp.float32(0.0)), axis=1)
-    damping = 1.0 / (1.0 + voxel_rate)
-    own = coupling.reshape(HALF, NZ, NX)
-    before = from_behind(own, ("vox", "col"), 1)
-    position = lax.axis_index(("vox", "col"))
-    device_count = lax.axis_size(("vox", "col"))
-    weights = row_weights(own, before, position == 0, position == device_count - 1, voxel_rate.reshape(NZ, NX))
-
-    modes, dirs = (
-        lax.all_to_all(start_modes, "col", split_axis=1, concat_axis=0, tiled=True),
-        lax.all_to_all(start_dirs, "col", split_axis=1, concat_axis=0, tiled=True),
-    )
-    count = modes.shape[0]
-    row, small = (count, local_voxels), (count, count)
-    images, dir_images, ritz = call_remote(
-        start_kernel, "start", 1, (row, row, small), 4, 128, [RITZ_LAYOUT], (modes, dirs, weights), 4
+    count = start_modes.shape[0] * 8
+    row, line, small = (count, local_voxels), (1, local_voxels), (count, count)
+    modes, dirs, images, dir_images, weights, damping, ritz = call_remote(
+        start_kernel, "start", 1, (row, row, row, row, (18, local_voxels), line, small),
+        [row, row, row, row, coupling.shape, small], [RITZ_LAYOUT],
+        (start_modes, start_dirs, coupling, relax_class[None, :], relaxivity[None, :]), 19,
     )
     ritz = symmetric(ritz)
     for iteration in range(ITERS):
         search, search_images, summed = call_remote(
-            search_kernel, "search", 2, (row, row, (12 * count, count)), 2, 12 * count, GRAM_LAYOUTS,
-            (modes, images, dirs, dir_images, ritz, damping[None, :], weights), 2,
+            search_kernel, "search", 2, (row, row, (GRAM_ROWS, count)), [row, row, (GRAM_ROWS, count)], GRAM_LAYOUTS,
+            (modes, images, dirs, dir_images, ritz, damping, weights), 2,
         )
-        basis = jnp.concatenate([modes, search, dirs], axis=0)
-        basis_images = jnp.concatenate([images, search_images, dir_images], axis=0)
         coeffs, ritz = solve_pencil(summed)
-        modes = matmul(coeffs.T, basis)
-        images = matmul(coeffs.T, basis_images)
-        dirs = matmul(coeffs[count:].T, basis[count:])
-        dir_images = matmul(coeffs[count:].T, basis_images[count:])
-    total_voxels = device_count * local_voxels
-    scaled = modes * math.sqrt(total_voxels)
-    modes_out = lax.all_to_all(scaled, "col", split_axis=0, concat_axis=1, tiled=True)
+        if iteration < ITERS - 1:
+            basis = jnp.concatenate([modes, search, dirs], axis=0)
+            basis_images = jnp.concatenate([images, search_images, dir_images], axis=0)
+            modes = matmul(coeffs.T, basis)
+            images = matmul(coeffs.T, basis_images)
+            dirs = matmul(coeffs[count:].T, basis[count:])
+            dir_images = matmul(coeffs[count:].T, basis_images[count:])
+    modes_out, = call_remote(
+        finish_kernel, "finish", 3, (start_modes.shape,), [row], [], (coeffs, modes, search, dirs), 7
+    )
     return (modes_out, ritz)
 
 

time: 281 us -> 247 us (0.88)
  starting transfers between devices: 13.6 us -> 0 us
  Pallas kernels: 230 us -> 240 us
  other arithmetic: 9.21 us -> 0.01 us
  blocking collectives: 8.97 us -> 0 us
  local copies, waits for them, and re-layouts: 12.2 us -> 4.12 us
  waiting for transfers between devices: 3.06 us -> 0 us
    pallas_call x3 -> x4, Pallas kernels: 112 us -> 122 us  [call_remote(): pl.pallas_call(kernel, out_shape=tuple((jax.ShapeDtypeStruct(shape, jnp.f...]
    all_to_all x2 -> x0, starting transfers between devices: 9.09 us -> none  [the longest x1 4.82 us: on_device(): lax.all_to_all(start_dirs, 'col', split_axis=1, concat_axis=0, tiled=True)]
    all_to_all x1 -> x0, blocking collectives: 8.97 us -> none  [on_device(): lax.all_to_all(scaled, 'col', split_axis=0, concat_axis=1, tiled=True)]
    concatenate x12 -> x0, other arithmetic: 8.41 us -> none  [row_weights(): rows += [jnp.roll(block.reshape(NZ * NX), dx) for block in (same, other)]]
    slice x18 -> x0, local copies, waits for them, and re-layouts: 7.22 us -> none  [row_weights(): rows += [jnp.roll(block.reshape(NZ * NX), dx) for block in (same, other)]]
    ppermute x1 -> x0, starting transfers between devices: 4.51 us -> none  [from_behind(): return lax.ppermute(block, axis, route)]
    unnamed x22 -> x11, local copies, waits for them, and re-layouts: 0.67 us -> 4.03 us
    all_to_all x3 -> x0, local copies, waits for them, and re-layouts: 3.1 us -> none  [the longest x1 1.67 us: on_device(): lax.all_to_all(start_modes, 'col', split_axis=1, concat_axis=0, tiled=True)]
  transfers between devices with their start and end apart: 3 -> 0, of which waited for: 1 -> 0; matrix products, arithmetic and copies ran while one was open for 7% -> 0% of each run, Pallas kernels for 0% -> 0%
where the time goes in v4:
time: 247 us
  Pallas kernels  240 us (97%)
  local copies, waits for them, and re-layouts  4.12 us (2%)
    pallas_call x4, Pallas kernels, call_remote(): pl.pallas_call(kernel, out_shape=tuple((jax.ShapeDtypeStruct(shape, jnp.f...  122 us
    pallas_call x2, Pallas kernels, solve_pencil(): pl.pallas_call(pencil_kernel, out_shape=(jax.ShapeDtypeStruct((3 * n, n),...  118 us

profile of v4, /device:TPU:1, one launch (start us, length us, event | category | flops | bytes accessed | tf_op | source)
XLA Modules:
  0.0 247.1 jit_solution(1709740844214419814)
XLA Ops:
  0.6 0.0 copy-start.3
  0.6 0.0 copy-start.4
  0.7 0.7 copy-done.3
  1.3 0.0 copy-done.4
  1.3 0.0 copy-start
  1.3 0.9 copy-done
  2.3 0.0 copy-start.1
  2.3 0.9 copy-done.1
  3.2 0.0 copy-start.2
  3.2 0.8 copy-done.2
  4.0 43.3 %start.1 = (f32[128,512]{1,0:T(8,128)S(1)}, f32[128,512]{1,0:T(8,128)S(1)}, f32[128,512]{1,0:T(8,128)S(1)}, f32[128,512]{1,0:T(8,128)S(1)}, f32[18,512]{1,0:T(8,...) custom-call(f32[16,4096]{1,0:T(8,128)S(1)} %copy-done, f32[16,4096]{1,0:T(8,128)S(1)} %copy-done.1, ...), custom_call_target="tpu_custom_call" | custom-call | tf_op jit(solution)/shard_map/start/pallas_call | solution.py:374
  47.3 0.1 copy.7
  47.4 35.6 %search.2 = (f32[128,512]{1,0:T(8,128)S(1)}, f32[128,512]{1,0:T(8,128)S(1)}, f32[1408,128]{1,0:T(8,128)S(1)}) custom-call(f32[128,512]{1,0:T(8,128)S(1)} %get-tuple-element.18.modes_ref, f32[128,512]{1,0:T(8,128)S(1)} %get-tuple-element.19.images_ref, f32[128,512]{1,0:T(8,128)S(1)} %get-tuple-element.20.dirs_ref, ...), custom_call_target="tpu_custom_call" | custom-call | tf_op jit(solution)/shard_map/search/pallas_call | solution.py:374
  83.1 98.5 %pencil.2 = (f32[384,128]{1,0:T(8,128)S(1)}, f32[128,128]{1,0:T(8,128)S(1)}) custom-call(f32[1408,128]{1,0:T(8,128)S(1)} %get-tuple-element.25.sum_ref), custom_call_target="tpu_custom_call" | custom-call | tf_op jit(solution)/shard_map/pencil/pallas_call | solution.py:532
  181.5 0.7 fusion.modes_ref
  182.2 0.5 fusion.12.dirs_ref
  182.7 0.7 fusion.6.images_ref
  183.3 0.5 fusion.16.dir_images_ref
  183.8 35.8 %search.3 = (f32[128,512]{1,0:T(8,128)S(1)}, f32[128,512]{1,0:T(8,128)}, f32[1408,128]{1,0:T(8,128)S(1)}) custom-call(f32[128,512]{1,0:T(8,128)S(1)} %fusion.modes_ref, f32[128,512]{1,0:T(8,128)S(1)} %fusion.6.images_ref, f32[128,512]{1,0:T(8,128)S(1)} %fusion.12.dirs_ref, f32[128,512]{1,0:T(8,128)S(1)} %fusion.16.dir_images_ref, ...), custom_call_target="tpu_custom_call" | custom-call | tf_op jit(solution)/shard_map/search/pallas_call | solution.py:374
  219.6 19.2 %pencil.3 = (f32[384,128]{1,0:T(8,128)S(1)}, f32[128,128]{1,0:T(8,128)}) custom-call(f32[1408,128]{1,0:T(8,128)S(1)} %get-tuple-element.30.sum_ref), custom_call_target="tpu_custom_call" | custom-call | tf_op jit(solution)/shard_map/pencil/pallas_call | solution.py:532
  238.8 7.6 %finish.1 = f32[16,4096]{1,0:T(8,128)S(1)} custom-call(f32[384,128]{1,0:T(8,128)S(1)} %get-tuple-element.31.coeff_ref, f32[128,512]{1,0:T(8,128)S(1)} %fusion.modes_ref, f32[128,512]{1,0:T(8,128)S(1)} %get-tuple-element.32.search_ref, f32[128,512]{1,0:T(8,128)S(1)} %fusion.12.dirs_ref), custom_call_target="tpu_custom_call" | custom-call | tf_op jit(solution)/shard_map/finish/pallas_call | solution.py:374
  246.4 0.7 copy.9
  (1 shorter events, 0.0 us)
Async XLA Ops:
  0.6 0.7 copy-start.3
  0.6 0.7 copy-start.4
  1.3 1.0 copy-start
  2.3 0.9 copy-start.1
  3.2 0.8 copy-start.2
